TPU v7x, 128 devices: a whole 4x4x4 slice. The times are simulated.
128 devices in a mesh: fsdp: 16 (over z, y), grp: 8 (over x, core).
Axes of the slice: x: 4, y: 4, z: 4, core: 2. Of those that a mesh axis runs over, the one named last changes fastest.
Arguments:
- tokens: bfloat16 [16384, 4096], P('fsdp'), may hold values from -6 to 6
- database: bfloat16 [128, 128, 896], P('fsdp'), may hold values from -6 to 6
- neighbour_ids: int32 [256, 2], P('fsdp'), may hold values from 0 to 127, as said below
- shard_map: int32 [128], replicated, may hold values from 0 to 127, as said below
- q_weight: bfloat16 [4096, 4096], P('fsdp', 'grp'), may hold values from -0.09375 to 0.09375
- k_weight: bfloat16 [896, 4096], P('fsdp', 'grp'), may hold values from -0.1875 to 0.1875
- v_weight: bfloat16 [896, 4096], P('fsdp', 'grp'), may hold values from -0.1875 to 0.1875
- o_weight: bfloat16 [4096, 4096], P('grp', 'fsdp'), may hold values from -0.75 to 0.75
Outputs:
- mixed: bfloat16 [16384, 4096], P(('fsdp', 'grp'))
Inputs may be any that keep to these rules, and one draw needn't show every extreme that they name: shard_map is a permutation: database span id i lies on index shard_map[i] // 8 of fsdp, as its local span shard_map[i] % 8. `neighbour_ids`: among the 32 neighbour ids of the spans of one index of fsdp, at most 4 lie on any one index of fsdp; in every draw one index of fsdp holds exactly 4 of them for every index's spans. Ids may repeat.
All inputs are finite; a program needn't handle non-finite values.
Results may differ from a plain program's by a relative error of at most 0.018.
Values may be sent and summed in bfloat16 or wider, within the bound.
No kernel may reach another device: no remote copies, remote signals or barrier semaphores. Data moves between devices by JAX's collectives and lax.ppermute only.
A program may use at most 128 MiB of HBM per device.

v0:
```python
import math

import jax
import jax.numpy as jnp
from jax import lax
from jax.sharding import PartitionSpec as P

HEAD = 128


norm_eps = 1e-06


def head_norm(field):
    shaped = field.reshape(field.shape[:-1] + (field.shape[-1] // HEAD, HEAD))
    scaled = shaped * lax.rsqrt(jnp.mean(shaped * shaped, axis=-1, keepdims=True) + norm_eps)
    return scaled.reshape(field.shape)


def project_rows(rows, k_panel, v_panel):
    flat_rows = rows.reshape(-1, rows.shape[-1])
    key_rows = head_norm(jnp.dot(flat_rows, k_panel, preferred_element_type=jnp.float32)).astype(
        jnp.bfloat16
    )
    value_rows = jnp.dot(flat_rows, v_panel, preferred_element_type=jnp.float32).astype(
        jnp.bfloat16
    )
    out_shape = rows.shape[:-1] + (k_panel.shape[1],)
    return (key_rows.reshape(out_shape), value_rows.reshape(out_shape))


def local(tokens, database, neighbour_ids, shard_map, q_weight, k_weight, v_weight, o_weight):
    devices = lax.axis_size("fsdp")
    span_count, neigh_count = neighbour_ids.shape
    wanted = span_count * neigh_count
    stored, row_len, enc_width = database.shape
    capacity = max(2, 4 * span_count // devices)
    slot_total = devices * capacity
    k_panel, v_panel = (
        lax.all_gather(k_weight, "fsdp", axis=0, tiled=True),
        lax.all_gather(v_weight, "fsdp", axis=0, tiled=True),
    )
    width = k_panel.shape[1]
    heads_here = width // HEAD
    flat_ids = neighbour_ids.reshape(wanted)
    id_range = jnp.arange(shard_map.shape[0], dtype=jnp.int32)
    position = jnp.sum(
        jnp.where(flat_ids[:, None] == id_range[None, :], shard_map[None, :], 0), axis=1
    )
    holder = position // stored
    local_index = position % stored
    order_index = jnp.arange(wanted, dtype=jnp.int32)
    earlier = (holder[:, None] == holder[None, :]) & (order_index[None, :] < order_index[:, None])
    slot_index = holder * capacity + jnp.sum(earlier, axis=1)
    slot_hits = slot_index[:, None] == jnp.arange(slot_total, dtype=jnp.int32)[None, :]
    ask_table = jnp.sum(jnp.where(slot_hits, local_index[:, None], 0), axis=0).reshape(
        devices, capacity
    )
    returned = lax.all_to_all(
        database[lax.all_to_all(ask_table, "fsdp", split_axis=0, concat_axis=0, tiled=True)],
        "fsdp",
        split_axis=0,
        concat_axis=0,
        tiled=True,
    )
    fetched = returned.reshape(slot_total, row_len, enc_width)[slot_index]
    key_rows, value_rows = project_rows(fetched, k_panel, v_panel)
    queries = jnp.dot(
        tokens,
        lax.all_gather(q_weight, "fsdp", axis=0, tiled=True),
        preferred_element_type=jnp.float32,
    )
    query_hat = head_norm(queries).astype(jnp.bfloat16)
    span_len = tokens.shape[0] // span_count
    query_blocks = query_hat.reshape(span_count, span_len, heads_here, HEAD)
    key_blocks = key_rows.reshape(span_count, neigh_count * row_len, heads_here, HEAD)
    value_blocks = value_rows.reshape(span_count, neigh_count * row_len, heads_here, HEAD)
    scores = jnp.einsum(
        "cqhd,ckhd->chqk", query_blocks, key_blocks, preferred_element_type=jnp.float32
    ) / math.sqrt(HEAD)
    raised = jnp.exp(scores)
    soft_weights = (raised / jnp.sum(raised, axis=-1, keepdims=True)).astype(jnp.bfloat16)
    attended = jnp.einsum(
        "chqk,ckhd->cqhd", soft_weights, value_blocks, preferred_element_type=jnp.float32
    )
    attended = attended.astype(jnp.bfloat16).reshape(tokens.shape[0], width)
    o_panel = lax.all_gather(o_weight, "fsdp", axis=1, tiled=True)
    return lax.psum_scatter(
        jnp.dot(attended, o_panel, preferred_element_type=jnp.float32).astype(jnp.bfloat16),
        "grp",
        scatter_dimension=0,
        tiled=True,
    )


def solution(mesh):
    in_specs = (
        P("fsdp", None),
        P("fsdp", None, None),
        P("fsdp", None),
        P(),
        P("fsdp", "grp"),
        P("fsdp", "grp"),
        P("fsdp", "grp"),
        P("grp", "fsdp"),
    )
    out_specs = P(("fsdp", "grp"), None)
    return jax.shard_map(local, mesh=mesh, in_specs=in_specs, out_specs=out_specs, check_vma=False)
```

profile of v0, /device:TPU:1, one launch (start us, length us, event | category | flops | bytes accessed | tf_op | source)
XLA Modules:
  0.0 435.8 jit_solution(7249427675671997436)
XLA Ops:
  6.5 0.9 copy.35
  7.4 0.1 eq.22
  7.5 0.8 select_reduce_fusion.1
  8.4 0.2 convert_reduce_fusion
  8.6 0.1 select_reduce_fusion
  8.7 0.1 all_to_all.11
  8.7 14.8 %all_to_all.17 = s32[16,1,4]{2,1,0:T(1,128)S(1)} all-to-all(s32[16,1,4]{2,1,0:T(1,128)S(1)} %bitcast.58), channel_id=1, replica_groups=mesh['fsdp'=16,'grp'=8] {'fsdp'}, dimensions={0} | all-to-all | bytes 512 | tf_op jit(solution)/shard_map/all_to_all | solution.py:60
  23.6 0.1 copy.37
  23.6 0.1 copy.38
  23.7 0.1 reshape.182
  23.8 8.3 %gather_fusion = bf16[64,128,896]{2,1,0:T(8,128)(2,1)} fusion(bf16[8,128,896]{2,1,0:T(8,128)(2,1)S(1)} %copy-done, s32[1024]{0:T(1024)S(1)} %pad_clamp_fusion.1), kind=kCustom, calls=%fused_computation | custom fusion | bytes 29360384 | tf_op jit(solution)/shard_map/gather | solution.py:60
  32.1 5.2 %all-to-all-start.1 = ((bf16[16,4,128,896]{3,2,1,0:T(8,128)(2,1)}), bf16[16,4,128,896]{3,2,1,0:T(8,128)(2,1)}, u32[]{:S(2)}, u32[]{:S(2)}) async-start(bf16[16,4,128,896]{3,2,1,0:T(8,128)(2,1)} %bitcast.51), calls=%async_computation.1 | async-start | bytes 29360128 | tf_op jit(solution)/shard_map/all_to_all | solution.py:59
  37.3 0.0 all-gather.3.cloned.1.call-start
  37.3 0.7 all-gather.3.cloned.1.call-update
  38.1 0.7 all-gather.5.cloned.1.call-update
  38.8 0.0 reduce-scatter.2.cloned.1.call-start
  38.8 245.9 %all_gather.14 = bf16[896,512]{1,0:T(8,128)(2,1)S(1)} all-gather(bf16[56,512]{1,0:T(8,128)(2,1)S(1)} %copy-done.5), channel_id=1, replica_groups=mesh['fsdp'=16,'grp'=8] {'fsdp'}, dimensions={0}, use_global_device_ids=true | all-gather | bytes 974848 | tf_op jit(solution)/shard_map/all_gather | solution.py:40
  284.7 0.6 copy.40
  285.3 21.4 %all_gather.12 = bf16[896,512]{1,0:T(8,128)(2,1)} all-gather(bf16[56,512]{1,0:T(8,128)(2,1)S(1)} %copy-done.6), channel_id=1, replica_groups=mesh['fsdp'=16,'grp'=8] {'fsdp'}, dimensions={0}, use_global_device_ids=true | all-gather | bytes 974848 | tf_op jit(solution)/shard_map/all_gather | solution.py:41
  306.8 8.5 %bitcast_reduce_fusion = (f32[1024,4]{0,1:T(4,128)S(1)}, f32[1024,512]{0,1:T(8,128)S(1)}) fusion(bf16[1024,4096]{1,0:T(8,128)(2,1)} %param.8, bf16[4096,512]{1,0:T(8,128)(2,1)} %all-gather.3.cloned.1.call-done), kind=kOutput, calls=%fused_computation.16 | convolution fusion | flops 4296011776 | bytes 14696448 | tf_op jit(solution)/shard_map/dot_general | solution.py:68
  315.3 0.3 fusion.6
  315.6 2.3 reshape.198
  317.9 9.9 %gather_fusion.1 = bf16[32,128,896]{2,1,0:T(8,128)(2,1)} fusion(bf16[64,128,896]{2,1,0:T(8,128)(2,1)} %bitcast.3, s32[1024]{0:T(1024)S(1)} %pad_clamp_fusion), kind=kCustom, calls=%fused_computation.1 | custom fusion | bytes 14680192 | tf_op jit(solution)/shard_map/gather | solution.py:66
  327.8 9.2 %convolution_convert_fusion.1 = bf16[4096,512]{1,0:T(8,128)(2,1)} fusion(bf16[4096,896]{1,0:T(8,128)(2,1)} %bitcast.53, bf16[896,512]{1,0:T(8,128)(2,1)S(1)} %copy-done.4), kind=kOutput, calls=%fused_computation.5 | convolution fusion | flops 3760193536 | bytes 12451840 | tf_op jit(solution)/shard_map/dot_general | solution.py:25
  337.0 7.0 %reshape_reshape.4 = bf16[16,256,4,128]{3,2,1,0:T(4,128)(2,1)} reshape(bf16[4096,512]{1,0:T(8,128)(2,1)} %convolution_convert_fusion.1) | data formatting | bytes 8388608 | tf_op jit(solution)/shard_map/reshape;reshape | solution.py:77
  344.0 8.3 %multiply_reduce_fusion = (f32[4096,4]{0,1:T(4,128)S(1)}, f32[4096,4,128]{2,0,1:T(8,128)S(1)}) fusion(bf16[4096,896,1]{1,0,2:T(8,128)(2,1)} %bitcast.54, bf16[4,128,896]{2,1,0:T(8,128)(2,1)S(1)} %bitcast.57), kind=kOutput, calls=%fused_computation.3 | convolution fusion | flops 3762274304 | bytes 16711680 | tf_op jit(solution)/shard_map/dot_general | solution.py:22
  352.3 2.7 multiply_convert_fusion
  355.0 2.5 fusion.4
  357.5 1.8 fusion.12
  359.2 0.9 copy.44
  360.2 8.9 %convolution_convert_fusion = bf16[1024,4096]{1,0:T(8,128)(2,1)} fusion(bf16[512,4096]{1,0:T(8,128)(2,1)} %all-gather.5.cloned.1.call-done, bf16[128,8,4,128]{3,2,1,0:T(4,128)(2,1)S(1)} %bitcast.56), kind=kOutput, calls=%fused_computation.4 | convolution fusion | flops 4299161600 | bytes 13631488 | tf_op jit(solution)/shard_map/dot_general | solution.py:89
  369.1 60.1 %reduce-scatter.2.cloned.1.call-done = bf16[128,4096]{1,0:T(8,128)(2,1)} async-done(((bf16[1024,4096]{1,0:T(8,128)(2,1)}), bf16[128,4096]{1,0:T(8,128)(2,1)}) %reduce-scatter.2.cloned.1.call-update) | async-done | bytes 1048592 | tf_op jit(solution)/shard_map/reduce_scatter | solution.py:88
  (27 shorter events, 0.2 us)
Async XLA Ops:
  6.5 17.3 %copy-start = (bf16[8,128,896]{2,1,0:T(8,128)(2,1)S(1)}, bf16[8,128,896]{2,1,0:T(8,128)(2,1)}, u32[]{:S(2)}) copy-start(bf16[8,128,896]{2,1,0:T(8,128)(2,1)} %param.9) | copy-start | bytes 5505028
  32.1 6.7 %copy-start.5 = (bf16[56,512]{1,0:T(8,128)(2,1)S(1)}, bf16[56,512]{1,0:T(8,128)(2,1)}, u32[]{:S(2)}) copy-start(bf16[56,512]{1,0:T(8,128)(2,1)} %param.13) | copy-start | bytes 172036
  32.1 253.2 %copy-start.6 = (bf16[56,512]{1,0:T(8,128)(2,1)S(1)}, bf16[56,512]{1,0:T(8,128)(2,1)}, u32[]{:S(2)}) copy-start(bf16[56,512]{1,0:T(8,128)(2,1)} %param.14) | copy-start | bytes 172036
  32.1 285.8 %all-to-all-start.1 = ((bf16[16,4,128,896]{3,2,1,0:T(8,128)(2,1)}), bf16[16,4,128,896]{3,2,1,0:T(8,128)(2,1)}, u32[]{:S(2)}, u32[]{:S(2)}) async-start(bf16[16,4,128,896]{3,2,1,0:T(8,128)(2,1)} %bitcast.51), calls=%async_computation.1 | async-start | bytes 29360128 | tf_op jit(solution)/shard_map/all_to_all | solution.py:59
  37.3 269.5 %all-gather.3.cloned.1.call-start = ((), (), s32[]{:S(2)}) async-start(), calls=%async_computation.3 | async-start | bytes 4456448 | tf_op jit(solution)/shard_map/all_gather | solution.py:70
  38.0 322.2 %all-gather.5.cloned.1.call-start = ((), (), s32[]{:S(2)}) async-start(), calls=%async_computation.4 | async-start | bytes 4456448 | tf_op jit(solution)/shard_map/all_gather | solution.py:87
  38.8 390.5 %reduce-scatter.2.cloned.1.call-start = ((), (), s32[]{:S(2)}) async-start(), calls=%async_computation.5 | async-start | bytes 9437184 | tf_op jit(solution)/shard_map/reduce_scatter | solution.py:88
  317.9 9.9 %copy-start.4 = (bf16[896,512]{1,0:T(8,128)(2,1)S(1)}, bf16[896,512]{1,0:T(8,128)(2,1)}, u32[]{:S(2)}) copy-start(bf16[896,512]{1,0:T(8,128)(2,1)} %all_gather.12) | copy-start | bytes 2752516
  352.3 2.7 copy-start.2
  355.0 2.5 copy-start.3
  369.1 60.2 %copy-start.1 = (bf16[8,128,896]{2,1,0:T(8,128)(2,1)S(1)}, bf16[8,128,896]{2,1,0:T(8,128)(2,1)}, u32[]{:S(2)}) copy-start(bf16[8,128,896]{2,1,0:T(8,128)(2,1)} %param.9) | copy-start | bytes 5505028
Sparse Core Ops, SparseCore 0:
  40.3 214.8 all-gather.2
  257.3 69.0 all-gather.4
  369.2 59.9 reduce-scatter.1
where the time goes:
time: 436 us
  blocking collectives  282 us (65%)
  waiting for transfers between devices  61.6 us (14%)
  matrix products  39 us (9%)
  local copies, waits for them, and re-layouts  30.3 us (7%)
  between operations  13.3 us (3%)
  starting transfers between devices  5.28 us (1%)
    all_gather x1, blocking collectives, local(): lax.all_gather(k_weight, 'fsdp', axis=0, tiled=True)  246 us
    reduce_scatter x1, waiting for transfers between devices, local(): lax.psum_scatter(jnp.dot(attended, o_panel, preferred_element_type=jnp.fl...  60.1 us
    all_gather x1, blocking collectives, local(): lax.all_gather(v_weight, 'fsdp', axis=0, tiled=True)  21.4 us
    all_to_all x1, blocking collectives, local(): lax.all_to_all(ask_table, 'fsdp', split_axis=0, concat_axis=0, tiled=True)  14.8 us
    gather x1, local copies, waits for them, and re-layouts, local(): fetched = returned.reshape(slot_total, row_len, enc_width)[slot_index]  9.92 us
    dot_general x1, matrix products, project_rows(): jnp.dot(flat_rows, v_panel, preferred_element_type=jnp.float32)  9.17 us
    dot_general x1, matrix products, local(): jnp.dot(attended, o_panel, preferred_element_type=jnp.float32)  8.9 us
  transfers between devices with their start and end apart: 4, of which 1 were waited for; matrix products, arithmetic and copies ran while one was open for 12% of the time, Pallas kernels for 0%

commit v1 on v0

v1 whole, which is shorter than its diff:
```python
import functools
import math

import jax
import jax.numpy as jnp
from jax import lax
from jax.experimental import pallas as pl
from jax.experimental.pallas import tpu as pltpu
from jax.sharding import PartitionSpec as P

HEAD = 128
EPS = 1e-06
RING = 4
ORDER = (0, 3, 1, 2)
PLACE = (0, 2, 3, 1)
VMEM_LIMIT = 56 * 1024 * 1024
ANY = pl.BlockSpec(memory_space=pl.ANY)
VMEM = pl.BlockSpec(memory_space=pltpu.VMEM)


def shift(value, axis, step):
    size = lax.axis_size(axis)
    return lax.ppermute(value, axis, [(i, (i + step) % size) for i in range(size)])


def gather_small(block, axis):
    return jnp.stack(
        [block, shift(block, axis, 1), shift(block, axis, -1), shift(block, axis, 2)]
    )


def gather_ring(blocks, axis):
    half = blocks.shape[0] // 2
    before, after = shift(blocks, axis, 1), shift(blocks, axis, -1)
    return [
        blocks,
        before,
        after,
        shift(before[:half], axis, 1),
        shift(after[half:], axis, -1),
    ]


def after(value, *earlier):
    return lax.optimization_barrier((value,) + earlier)[0]


BLOCKS = tuple((p, s) for p in range(3) for s in range(4)) + ((3, 0), (3, 1), (4, 0), (4, 1))


def block_owners(z, y):
    major = jnp.array([ORDER[k // 4] for k in range(16)], jnp.int32)
    minor = jnp.array([ORDER[k % 4] for k in range(16)], jnp.int32)
    by_zy = ((z + minor) % RING) * RING + (y + major) % RING
    by_yz = ((z + major) % RING) * RING + (y + minor) % RING
    return by_zy.astype(jnp.int32), by_yz.astype(jnp.int32)


def pick_kernel(place_ref, *refs):
    pieces, (out_ref, sem) = refs[:5], refs[5:]
    bounds = (0, 32, 64, 96, 112, 128)

    def one(j, carry):
        place = place_ref[j]
        for low, high, piece in zip(bounds[:-1], bounds[1:], pieces):

            @pl.when((place >= low) & (place < high))
            def _():
                pltpu.make_async_copy(piece.at[place - low], out_ref.at[j], sem).start()

        return carry

    lax.fori_loop(0, out_ref.shape[0], one, 0)
    pltpu.make_async_copy(out_ref, out_ref, sem).wait()


def pick(place, pieces, count):
    shape = pieces[0].shape[1:]
    return pl.pallas_call(
        pick_kernel,
        out_shape=jax.ShapeDtypeStruct((count,) + shape, jnp.bfloat16),
        grid_spec=pltpu.PrefetchScalarGridSpec(
            num_scalar_prefetch=1,
            grid=(1,),
            in_specs=[ANY] * 5,
            out_specs=VMEM,
            scratch_shapes=[pltpu.SemaphoreType.DMA],
        ),
        cost_estimate=pl.CostEstimate(flops=0, bytes_accessed=2 * 1024 * 1024, transcendentals=0),
        name="pick",
    )(place, *pieces)


def arrange_kernel(owner_ref, *refs):
    pieces, (out_ref, sem) = refs[:5], refs[5:]
    for k, (p, s) in enumerate(BLOCKS):
        pltpu.make_async_copy(pieces[p].at[s], out_ref.at[owner_ref[k]], sem).start()
    pltpu.make_async_copy(out_ref, out_ref, sem).wait()


def arrange(owners, pieces):
    return pl.pallas_call(
        arrange_kernel,
        out_shape=jax.ShapeDtypeStruct((16,) + pieces[0].shape[1:], jnp.bfloat16),
        grid_spec=pltpu.PrefetchScalarGridSpec(
            num_scalar_prefetch=1,
            grid=(1,),
            in_specs=[ANY] * 5,
            out_specs=VMEM,
            scratch_shapes=[pltpu.SemaphoreType.DMA],
        ),
        cost_estimate=pl.CostEstimate(flops=0, bytes_accessed=4 * 1024 * 1024, transcendentals=0),
        name="arrange",
    )(owners, *pieces)


def normed(field):
    parts = []
    for h in range(field.shape[1] // HEAD):
        part = field[:, h * HEAD : (h + 1) * HEAD]
        scale = lax.rsqrt(jnp.mean(part * part, axis=-1, keepdims=True) + EPS)
        parts.append((part * scale).astype(jnp.bfloat16))
    return parts


def query_kernel(owner_ref, tokens_ref, *refs):
    pieces, (out_ref, weight_ref, sem) = refs[:5], refs[5:]

    @pl.when(pl.program_id(0) == 0)
    def _():
        for k, (p, s) in enumerate(BLOCKS):
            rows = pl.multiple_of(owner_ref[k] * 256, 256)
            pltpu.make_async_copy(
                pieces[p].at[s], weight_ref.at[pl.ds(rows, 256), :], sem
            ).start()
        pltpu.make_async_copy(weight_ref, weight_ref, sem).wait()

    field = jnp.dot(tokens_ref[...], weight_ref[...], preferred_element_type=jnp.float32)
    for h, part in enumerate(normed(field)):
        out_ref[:, h * HEAD : (h + 1) * HEAD] = part


def query_projection(owners, tokens, pieces):
    rows, depth = tokens.shape
    width = pieces[0].shape[2]
    block = 256
    return pl.pallas_call(
        query_kernel,
        out_shape=jax.ShapeDtypeStruct((rows, width), jnp.bfloat16),
        grid_spec=pltpu.PrefetchScalarGridSpec(
            num_scalar_prefetch=1,
            grid=(rows // block,),
            in_specs=[pl.BlockSpec((block, depth), lambda i, s: (i, 0))] + [ANY] * 5,
            out_specs=pl.BlockSpec((block, width), lambda i, s: (i, 0)),
            scratch_shapes=[
                pltpu.VMEM((depth, width), jnp.bfloat16),
                pltpu.SemaphoreType.DMA,
            ],
        ),
        compiler_params=pltpu.CompilerParams(vmem_limit_bytes=VMEM_LIMIT),
        cost_estimate=pl.CostEstimate(
            flops=2 * rows * depth * width, bytes_accessed=14 * 1024 * 1024, transcendentals=0
        ),
        name="query_projection",
    )(owners, tokens, *pieces)


def rows_kernel(mine_ref, other_ref, panel_ref, k_ref, v_ref):
    near, share, depth = mine_ref.shape
    half = k_ref.shape[-1]
    rows = jnp.concatenate([mine_ref[...], other_ref[...]], axis=1)
    rows = rows.reshape(near * 2 * share, depth)
    keys = jnp.dot(rows, panel_ref[:, :half], preferred_element_type=jnp.float32)
    values = jnp.dot(rows, panel_ref[:, half:], preferred_element_type=jnp.float32)
    for h, part in enumerate(normed(keys)):
        k_ref[:, :, h * HEAD : (h + 1) * HEAD] = part.reshape(near, 2 * share, HEAD)
    v_ref[...] = values.astype(jnp.bfloat16).reshape(near, 2 * share, half)


def project_rows(mine, other, panel):
    near, share, depth = mine.shape
    width = panel.shape[1] // 2
    block = 8
    shape = jax.ShapeDtypeStruct((near, 2 * share, width), jnp.bfloat16)
    spec = pl.BlockSpec((block, share, depth), lambda i: (i, 0, 0))
    out_spec = pl.BlockSpec((block, 2 * share, width), lambda i: (i, 0, 0))
    return pl.pallas_call(
        rows_kernel,
        out_shape=(shape, shape),
        grid=(near // block,),
        in_specs=[spec, spec, VMEM],
        out_specs=(out_spec, out_spec),
        compiler_params=pltpu.CompilerParams(vmem_limit_bytes=VMEM_LIMIT),
        cost_estimate=pl.CostEstimate(
            flops=4 * near * 2 * share * depth * width,
            bytes_accessed=6 * 1024 * 1024,
            transcendentals=0,
        ),
        name="project_rows",
    )(mine, other, panel)


def attend_kernel(query_ref, *refs):
    k_refs, v_refs, out_ref = refs[:4], refs[4:8], refs[8]
    heads = out_ref.shape[1] // HEAD
    spans, span, near = out_ref.shape[0] // 64, 64, 2
    scale = math.log2(math.e) / math.sqrt(HEAD)

    def of_span(piece_refs, s, lanes):
        rows = [r[s * near : (s + 1) * near, :, lanes].reshape(-1, HEAD) for r in piece_refs]
        return jnp.concatenate(rows, axis=0)

    pairs = [(s, slice(h * HEAD, (h + 1) * HEAD)) for s in range(spans) for h in range(heads)]
    scores = [
        lax.dot_general(
            query_ref[s * span : (s + 1) * span, lanes],
            of_span(k_refs, s, lanes),
            (((1,), (1,)), ((), ())),
            preferred_element_type=jnp.float32,
        )
        for s, lanes in pairs
    ]
    raised = [jnp.exp2(score * scale) for score in scores]
    sums = [jnp.sum(r, axis=-1, keepdims=True) for r in raised]
    for (s, lanes), r, total in zip(pairs, raised, sums):
        mixed = jnp.dot(
            r.astype(jnp.bfloat16), of_span(v_refs, s, lanes), preferred_element_type=jnp.float32
        )
        out_ref[s * span : (s + 1) * span, lanes] = (mixed / total).astype(jnp.bfloat16)


def attend(query, keys, values):
    rows, width = query.shape
    spans = 2
    block = spans * 64
    near = spans * 2
    piece = keys[0].shape
    return pl.pallas_call(
        attend_kernel,
        out_shape=jax.ShapeDtypeStruct((rows, width), jnp.bfloat16),
        grid=(rows // block,),
        in_specs=[pl.BlockSpec((block, width), lambda i: (i, 0))]
        + [pl.BlockSpec((near,) + piece[1:], lambda i: (i, 0, 0))] * 8,
        out_specs=pl.BlockSpec((block, width), lambda i: (i, 0)),
        compiler_params=pltpu.CompilerParams(vmem_limit_bytes=VMEM_LIMIT),
        cost_estimate=pl.CostEstimate(
            flops=4_000_000_000, bytes_accessed=12 * 1024 * 1024, transcendentals=4_000_000
        ),
        name="attend",
    )(query, *keys, *values)


def mix_kernel(turn_ref, mine_ref, other_ref, *refs):
    mine_w, other_w, outs = refs[:5], refs[5:10], refs[10:]
    rows = mine_ref.shape[1]
    order = [turn_ref[k] for k in (2, 1, 3, 0)]
    mine = jnp.concatenate([mine_ref[t] for t in order], axis=0)
    other = jnp.concatenate([other_ref[t] for t in order], axis=0)
    for j, (p, s) in enumerate(BLOCKS):
        total = jnp.dot(mine, mine_w[p][s], preferred_element_type=jnp.float32)
        total += jnp.dot(other, other_w[p][s], preferred_element_type=jnp.float32)
        total = total.astype(jnp.bfloat16)
        at = j % 8 * 256
        for k in range(4):
            outs[k * 2 + j // 8][:, at : at + 256] = total[k * rows : (k + 1) * rows]


def mix(turn, mine, other, mine_w, other_w):
    shape = jax.ShapeDtypeStruct((128, 2048), jnp.bfloat16)
    return pl.pallas_call(
        mix_kernel,
        out_shape=[shape] * 8,
        grid_spec=pltpu.PrefetchScalarGridSpec(
            num_scalar_prefetch=1,
            grid=(1,),
            in_specs=[VMEM] * 12,
            out_specs=[VMEM] * 8,
        ),
        compiler_params=pltpu.CompilerParams(vmem_limit_bytes=VMEM_LIMIT),
        cost_estimate=pl.CostEstimate(
            flops=2 * 512 * 1024 * 4096, bytes_accessed=14 * 1024 * 1024, transcendentals=0
        ),
        name="mix",
    )(turn, mine, other, *mine_w, *other_w)


def final_kernel(owner_ref, *refs):
    ins, out_ref = refs[:6], refs[6]
    for j in range(16):
        lanes = slice(j % 8 * 256, (j % 8 + 1) * 256)
        total = sum(ins[j // 8 * 3 + i][:, lanes].astype(jnp.float32) for i in range(3))
        at = pl.multiple_of(owner_ref[j] * 256, 256)
        out_ref[:, pl.ds(at, 256)] = total.astype(jnp.bfloat16)


def final(owners, parts):
    return pl.pallas_call(
        final_kernel,
        out_shape=jax.ShapeDtypeStruct((128, 4096), jnp.bfloat16),
        grid_spec=pltpu.PrefetchScalarGridSpec(
            num_scalar_prefetch=1, grid=(1,), in_specs=[VMEM] * 6, out_specs=VMEM
        ),
        compiler_params=pltpu.CompilerParams(vmem_limit_bytes=VMEM_LIMIT),
        name="final",
    )(owners, *parts)


def added(a, b):
    return (a.astype(jnp.float32) + b.astype(jnp.float32)).astype(jnp.bfloat16)


def local(tokens, database, neighbour_ids, shard_map, q_weight, k_weight, v_weight, o_weight):
    z, y, x, core = (lax.axis_index(a) for a in ("z", "y", "x", "core"))
    by_zy, by_yz = block_owners(z, y)
    stored = database.shape[0]

    ids = neighbour_ids.reshape(-1)
    span_ids = jnp.arange(shard_map.shape[0], dtype=jnp.int32)
    at = jnp.sum(jnp.where(ids[:, None] == span_ids[None, :], shard_map[None, :], 0), axis=1)
    owner, index = at // stored, at % stored
    dz, dy = (owner // RING - z) % RING, (owner % RING - y) % RING
    place_of = lambda d: jnp.where(d == 0, 0, jnp.where(d == 3, 1, d + 1))
    place = ((place_of(dy) * RING + place_of(dz)) * stored + index).astype(jnp.int32)

    share = lax.dynamic_slice_in_dim(database, (x * 2 + core) * 16, 16, axis=1)
    near_z = gather_small(share, "z")
    kv_y = gather_small(jnp.concatenate([k_weight, v_weight], axis=1), "y")
    q_y = gather_small(q_weight, "y")
    all_rows = gather_ring(near_z, "y")
    kv_all = gather_ring(after(kv_y, near_z), "z")
    o_z = gather_small(after(o_weight, near_z), "z")
    q_all = gather_ring(after(q_y, o_z), "z")
    o_all = gather_ring(after(o_z, *all_rows), "y")

    flat = [p.reshape((-1,) + p.shape[2:]) for p in all_rows]
    wanted = pick(place, flat, ids.shape[0])

    ring = gather_ring(wanted, "x")
    rings = ring[:3] + [jnp.concatenate(ring[3:], axis=0)]
    others = [shift(r, "core", 1) for r in rings]

    blocks = arrange(by_yz, kv_all)
    panel = blocks.reshape(-1, blocks.shape[-1])
    keys, values = zip(*[project_rows(a, b, panel) for a, b in zip(rings, others)])
    query = query_projection(by_yz, tokens, q_all)
    attended = attend(query, keys, values)

    o_other = [shift(w, "core", 1) for w in o_all]
    by_core = attended.reshape(4, 2, 128, attended.shape[1])
    mine = lax.dynamic_index_in_dim(by_core, core, axis=1, keepdims=False)
    give = lax.dynamic_index_in_dim(by_core, 1 - core, axis=1, keepdims=False)
    other = shift(give, "core", 1)
    turn = ((x + jnp.arange(4)) % RING).astype(jnp.int32)
    t2a, t2b, t1a, t1b, t3a, t3b, t0a, t0b = mix(turn, mine, other, o_all, o_other)

    to_next, to_last = shift(t2a, "x", 1), shift(t2b, "x", -1)
    r1b, r3a = shift(t1b, "x", 1), shift(t3a, "x", -1)
    r1a = shift(added(t1a, to_next), "x", 1)
    r3b = shift(added(t3b, to_last), "x", -1)
    return final(by_zy, [t0a, r1a, r3a, t0b, r1b, r3b])


def solution(mesh):
    grid = jax.sharding.Mesh(mesh.devices.reshape(4, 4, 4, 2), ("z", "y", "x", "core"))
    fsdp, grp = ("z", "y"), ("x", "core")
    in_specs = (
        P(fsdp, None),
        P(fsdp, None, None),
        P(fsdp, None),
        P(),
        P(fsdp, grp),
        P(fsdp, grp),
        P(fsdp, grp),
        P(grp, fsdp),
    )
    out_specs = P(fsdp + grp, None)
    return jax.shard_map(local, mesh=grid, in_specs=in_specs, out_specs=out_specs, check_vma=False)
```

time: 436 us -> 250 us (0.57)
  blocking collectives: 282 us -> 0 us
  Pallas kernels: 0 us -> 64.1 us
  starting transfers between devices: 5.28 us -> 65.3 us
  matrix products: 39 us -> 0 us
  waiting for transfers between devices: 61.6 us -> 95 us
  local copies, waits for them, and re-layouts: 30.3 us -> 15 us
  between operations: 13.3 us -> 0.55 us
  other arithmetic: 4.15 us -> 8.68 us
    all_gather x2 -> x0, blocking collectives: 267 us -> none  [the longest x1 246 us: local(): lax.all_gather(k_weight, 'fsdp', axis=0, tiled=True)]
    ppermute x0 -> x48, waiting for transfers between devices: none -> 95 us  [shift(): lax.ppermute(value, axis, [(i, (i + step) % size) for i in range(size)])]
    ppermute x0 -> x48, starting transfers between devices: none -> 65.3 us  [shift(): lax.ppermute(value, axis, [(i, (i + step) % size) for i in range(size)])]
    pallas_call x0 -> x10, Pallas kernels: none -> 64.1 us  [the longest x4 23.4 us: project_rows(): pl.pallas_call(rows_kernel, out_shape=(shape, shape), grid=(near // block...]
    reduce_scatter x1 -> x0, waiting for transfers between devices: 60.1 us -> none  [local(): lax.psum_scatter(jnp.dot(attended, o_panel, preferred_element_type=jnp.fl...]
    dot_general x6 -> x0, matrix products: 39 us -> none  [the longest x1 9.17 us: project_rows(): jnp.dot(flat_rows, v_panel, preferred_element_type=jnp.float32)]
    gather x2 -> x0, local copies, waits for them, and re-layouts: 18.2 us -> none  [the longest x1 9.92 us: local(): fetched = returned.reshape(slot_total, row_len, enc_width)[slot_index]]
    all_to_all x1 -> x0, blocking collectives: 14.8 us -> none  [local(): lax.all_to_all(ask_table, 'fsdp', split_axis=0, concat_axis=0, tiled=True)]
  transfers between devices with their start and end apart: 4 -> 48, of which waited for: 1 -> 13; matrix products, arithmetic and copies ran while one was open for 12% -> 7% of each run, Pallas kernels for 0% -> 20%
where the time goes in v1:
time: 250 us; the launch traced here: 249 us
  waiting for transfers between devices  95 us (38%)
  starting transfers between devices  65.3 us (26%)
  Pallas kernels  64.1 us (26%)
  local copies, waits for them, and re-layouts  15 us (6%)
  other arithmetic  8.68 us (3%)
    ppermute x48, waiting for transfers between devices, shift(): lax.ppermute(value, axis, [(i, (i + step) % size) for i in range(size)])  95 us
    ppermute x48, starting transfers between devices, shift(): lax.ppermute(value, axis, [(i, (i + step) % size) for i in range(size)])  65.3 us
    pallas_call x4, Pallas kernels, project_rows(): pl.pallas_call(rows_kernel, out_shape=(shape, shape), grid=(near // block...  23.4 us
    pallas_call x1, Pallas kernels, query_projection(): pl.pallas_call(query_kernel, out_shape=jax.ShapeDtypeStruct((rows, width)...  11.3 us
    pallas_call x1, Pallas kernels, mix(): pl.pallas_call(mix_kernel, out_shape=[shape] * 8, grid_spec=pltpu.Prefetc...  10.6 us
    pallas_call x1, Pallas kernels, attend(): pl.pallas_call(attend_kernel, out_shape=jax.ShapeDtypeStruct((rows, width...  8.54 us
    unnamed x85, local copies, waits for them, and re-layouts  6.55 us
    another operation x4, other arithmetic, gather_small(): jnp.stack([block, shift(block, axis, 1), shift(block, axis, -1), shift(bl...  5.47 us
  transfers between devices with their start and end apart: 48, of which 13 were waited for; matrix products, arithmetic and copies ran while one was open for 7% of the time, Pallas kernels for 20%

profile of v1, /device:TPU:1, one launch (start us, length us, event | category | flops | bytes accessed | tf_op | source)
XLA Modules:
  0.0 248.7 jit_solution(10511210149741838314)
XLA Ops:
  1.5 4.5 %collective-permute-start.5 = (bf16[8,16,896]{2,1,0:T(8,128)(2,1)S(1)}, bf16[8,16,896]{2,1,0:T(8,128)(2,1)S(1)}, u32[]{:S(2)}, u32[]{:S(2)}) collective-permute-start(bf16[8,16,896]{2,1,0:T(8,128)(2,1)S(1)} %constant_dynamic-slice_fusion), channel_id=1, source_target_pairs={{0,64},{32,96},{64,0},{96,32},{1,65},{33,97},{65,1},{97,33},{2,66}... | collective-permute-start | bytes 688136 | tf_op jit(solution)/shard_map/ppermute | solution.py:23
  7.5 3.8 %collective-permute-done.5 = bf16[8,16,896]{2,1,0:T(8,128)(2,1)S(1)} collective-permute-done((bf16[8,16,896]{2,1,0:T(8,128)(2,1)S(1)}, bf16[8,16,896]{2,1,0:T(8,128)(2,1)S(1)}, u32[]{:S(2)}, u32[]{:S(2)}) %collective-permute-start.5) | collective-permute-done | bytes 229408 | tf_op jit(solution)/shard_map/ppermute | solution.py:23
  11.4 5.4 %collective-permute-done.4 = bf16[8,16,896]{2,1,0:T(8,128)(2,1)S(1)} collective-permute-done((bf16[8,16,896]{2,1,0:T(8,128)(2,1)S(1)}, bf16[8,16,896]{2,1,0:T(8,128)(2,1)S(1)}, u32[]{:S(2)}, u32[]{:S(2)}) %collective-permute-start.4) | collective-permute-done | bytes 229408 | tf_op jit(solution)/shard_map/ppermute | solution.py:23
  23.5 22.1 %collective-permute-done.2 = bf16[256,512]{1,0:T(8,128)(2,1)} collective-permute-done((bf16[256,512]{1,0:T(8,128)(2,1)S(1)}, bf16[256,512]{1,0:T(8,128)(2,1)}, u32[]{:S(2)}, u32[]{:S(2)}) %collective-permute-start.2) | collective-permute-done | bytes 262176 | tf_op jit(solution)/shard_map/ppermute | solution.py:23
  45.6 4.3 %collective-permute-start.8 = (bf16[512,256]{1,0:T(8,128)(2,1)S(1)}, bf16[512,256]{1,0:T(8,128)(2,1)S(1)}, u32[]{:S(2)}, u32[]{:S(2)}) collective-permute-start(bf16[512,256]{1,0:T(8,128)(2,1)S(1)} %copy-done.17), channel_id=1, source_target_pairs={{0,64},{32,96},{64,0},{96,32},{1,65},{33,97},{65,1},{97,33},{2,66}... | collective-permute-start | bytes 786440 | tf_op jit(solution)/shard_map/ppermute | solution.py:23
  49.9 4.1 %collective-permute-start.7 = (bf16[512,256]{1,0:T(8,128)(2,1)S(1)}, bf16[512,256]{1,0:T(8,128)(2,1)}, u32[]{:S(2)}, u32[]{:S(2)}) collective-permute-start(bf16[512,256]{1,0:T(8,128)(2,1)S(1)} %copy-done.17), channel_id=1, source_target_pairs={{0,96},{32,0},{64,32},{96,64},{1,97},{33,1},{65,33},{97,65},{2,98}... | collective-permute-start | bytes 786440 | tf_op jit(solution)/shard_map/ppermute | solution.py:23
  55.7 2.2 pad_maximum_fusion.refs_0_
  57.9 2.6 %collective-permute-start.20 = (bf16[56,1024]{1,0:T(8,128)(2,1)}, bf16[56,1024]{1,0:T(8,128)(2,1)S(1)}, u32[]{:S(2)}, u32[]{:S(2)}) collective-permute-start(bf16[56,1024]{1,0:T(8,128)(2,1)} %constant_dynamic-update-slice_fusion), channel_id=1, source_target_pairs={{0,16},{8,24},{16,0},{24,8},{1,17},{9,25},{17,1},{25,9},{2,18},{10... | collective-permute-start | bytes 344072 | tf_op jit(solution)/shard_map/ppermute | solution.py:23
  65.0 2.2 pad_maximum_fusion.1.refs_0_
  69.0 2.2 collective-permute-start.10
  71.8 4.7 %collective-permute-done.15 = bf16[2,8,16,896]{3,2,1,0:T(8,128)(2,1)S(1)} collective-permute-done((bf16[2,8,16,896]{3,2,1,0:T(8,128)(2,1)S(1)}, bf16[2,8,16,896]{3,2,1,0:T(8,128)(2,1)S(1)}, u32[]{:S(2)}, u32[]{:S(2)}) %collective-permute-start.15) | collective-permute-done | bytes 458784 | tf_op jit(solution)/shard_map/ppermute | solution.py:23
  77.5 3.1 %pick.1.mine_ref = bf16[32,16,896]{2,1,0:T(8,128)(2,1)} custom-call(s32[32]{0:T(128)} %fusion.2.place_ref, bf16[32,16,896]{2,1,0:T(8,128)(2,1)} %bitcast.32, bf16[32,16,896]{2,1,0:T(8,128)(2,1)} %bitcast.33, bf16[32,16,896]{2,1,0:T(8,128)(2,1)} %bitcast.34, bf16[16,16,896]{2,1,0:T(8,128)(2,1)} %bitcast.40, bf16[16,16,896]{2,1,0:T(8,128)(2,1)} %bitcast.41), custom_call_target="tpu_custom_call" | custom-call | bytes 2097152 | tf_op jit(solution)/shard_map/pick/pallas_call | solution.py:79
  83.3 16.5 %collective-permute-done.21.refs_1_ = bf16[4,56,1024]{2,1,0:T(8,128)(2,1)S(1)} collective-permute-done((bf16[4,56,1024]{2,1,0:T(8,128)(2,1)S(1)}, bf16[4,56,1024]{2,1,0:T(8,128)(2,1)S(1)}, u32[]{:S(2)}, u32[]{:S(2)}) %collective-permute-start.21) | collective-permute-done | bytes 458784 | tf_op jit(solution)/shard_map/ppermute | solution.py:23
  102.6 5.0 %collective-permute-done.22.refs_2_ = bf16[4,56,1024]{2,1,0:T(8,128)(2,1)S(1)} collective-permute-done((bf16[4,56,1024]{2,1,0:T(8,128)(2,1)S(1)}, bf16[4,56,1024]{2,1,0:T(8,128)(2,1)S(1)}, u32[]{:S(2)}, u32[]{:S(2)}) %collective-permute-start.22) | collective-permute-done | bytes 458784 | tf_op jit(solution)/shard_map/ppermute | solution.py:23
  109.6 3.4 %collective-permute-start.12 = (bf16[2,256,512]{2,1,0:T(8,128)(2,1)S(1)}, bf16[2,256,512]{2,1,0:T(8,128)(2,1)S(1)}, u32[]{:S(2)}, u32[]{:S(2)}) collective-permute-start(bf16[2,256,512]{2,1,0:T(8,128)(2,1)S(1)} %slice.41), channel_id=1, source_target_pairs={{0,96},{32,0},{64,32},{96,64},{1,97},{33,1},{65,33},{97,65},{2,98}... | collective-permute-start | bytes 1572872 | tf_op jit(solution)/shard_map/ppermute | solution.py:23
  116.9 7.6 %collective-permute-done.24.refs_4_ = bf16[2,56,1024]{2,1,0:T(8,128)(2,1)S(1)} collective-permute-done((bf16[2,56,1024]{2,1,0:T(8,128)(2,1)S(1)}, bf16[2,56,1024]{2,1,0:T(8,128)(2,1)S(1)}, u32[]{:S(2)}, u32[]{:S(2)}) %collective-permute-start.24) | collective-permute-done | bytes 229408 | tf_op jit(solution)/shard_map/ppermute | solution.py:23
  124.5 2.5 collective-permute-start.30
  127.1 7.0 %collective-permute-start.17 = (bf16[32,16,896]{2,1,0:T(8,128)(2,1)}, bf16[32,16,896]{2,1,0:T(8,128)(2,1)}, u32[]{:S(2)}, u32[]{:S(2)}) collective-permute-start(bf16[32,16,896]{2,1,0:T(8,128)(2,1)} %pick.1.mine_ref), channel_id=1, source_target_pairs={{0,1},{1,0},{2,3},{3,2},{4,5},{5,4},{6,7},{7,6},{8,9},{9,8},{10,11... | collective-permute-start | bytes 2752520 | tf_op jit(solution)/shard_map/ppermute | solution.py:23
  135.5 3.4 %arrange.1 = bf16[16,56,1024]{2,1,0:T(8,128)(2,1)} custom-call(s32[16]{0:T(128)} %get-tuple-element.47.owner_ref, bf16[4,56,1024]{2,1,0:T(8,128)(2,1)} %copy-done.5, bf16[4,56,1024]{2,1,0:T(8,128)(2,1)} %copy-done.7, bf16[4,56,1024]{2,1,0:T(8,128)(2,1)} %copy-done.8, bf16[2,56,1024]{2,1,0:T(8,128)(2,1)} %copy-done.22, bf16[2,56,1024]{2,1,0:T(8,128)(2,1)} %copy-done.23), custom_call_target="tpu_custom_call" | custom-call | bytes 4194304 | tf_op jit(solution)/shard_map/arrange/pallas_call | solution.py:102
  139.7 11.3 %query_projection.1.query_ref = bf16[1024,512]{1,0:T(8,128)(2,1)} custom-call(s32[16]{0:T(128)} %get-tuple-element.47.owner_ref, bf16[1024,4096]{1,0:T(8,128)(2,1)} %tokens_ref.1, bf16[4,256,512]{2,1,0:T(8,128)(2,1)} %pad_maximum_fusion.refs_0_, bf16[4,256,512]{2,1,0:T(8,128)(2,1)} %collective-permute-done.9.refs_1_, ...), custom_call_target="tpu_custom_call" | custom-call | flops 4294967296 | bytes 14680064 | tf_op jit(solution)/shard_map/query_projection/pallas_call | solution.py:147
  156.5 5.8 %project_rows.4 = (bf16[32,32,512]{2,1,0:T(8,128)(2,1)}, bf16[32,32,512]{2,1,0:T(8,128)(2,1)}) custom-call(bf16[32,16,896]{2,1,0:T(8,128)(2,1)} %pick.1.mine_ref, bf16[32,16,896]{2,1,0:T(8,128)(2,1)} %collective-permute-done.17.other_ref, bf16[896,1024]{1,0:T(8,128)(2,1)} %bitcast.35), custom_call_target="tpu_custom_call" | custom-call | flops 1879048192 | bytes 6291456 | tf_op jit(solution)/shard_map/project_rows/pallas_call | solution.py:187
  162.4 5.9 %project_rows.5 = (bf16[32,32,512]{2,1,0:T(8,128)(2,1)}, bf16[32,32,512]{2,1,0:T(8,128)(2,1)}) custom-call(bf16[32,16,896]{2,1,0:T(8,128)(2,1)} %collective-permute-done.25.mine_ref, bf16[32,16,896]{2,1,0:T(8,128)(2,1)} %collective-permute-done.26.other_ref, bf16[896,1024]{1,0:T(8,128)(2,1)} %bitcast.36), custom_call_target="tpu_custom_call" | custom-call | flops 1879048192 | bytes 6291456 | tf_op jit(solution)/shard_map/project_rows/pallas_call | solution.py:187
  169.2 5.8 %project_rows.6 = (bf16[32,32,512]{2,1,0:T(8,128)(2,1)}, bf16[32,32,512]{2,1,0:T(8,128)(2,1)}) custom-call(bf16[32,16,896]{2,1,0:T(8,128)(2,1)} %copy-done.20, bf16[32,16,896]{2,1,0:T(8,128)(2,1)} %copy-done.33, bf16[896,1024]{1,0:T(8,128)(2,1)} %bitcast.37), custom_call_target="tpu_custom_call" | custom-call | flops 1879048192 | bytes 6291456 | tf_op jit(solution)/shard_map/project_rows/pallas_call | solution.py:187
  176.7 5.8 %project_rows.7 = (bf16[32,32,512]{2,1,0:T(8,128)(2,1)}, bf16[32,32,512]{2,1,0:T(8,128)(2,1)}) custom-call(bf16[32,16,896]{2,1,0:T(8,128)(2,1)} %copy-done.21, bf16[32,16,896]{2,1,0:T(8,128)(2,1)} %copy-done.32, bf16[896,1024]{1,0:T(8,128)(2,1)} %bitcast.38), custom_call_target="tpu_custom_call" | custom-call | flops 1879048192 | bytes 6291456 | tf_op jit(solution)/shard_map/project_rows/pallas_call | solution.py:187
  182.6 8.5 %attend.1 = bf16[1024,512]{1,0:T(8,128)(2,1)} custom-call(bf16[1024,512]{1,0:T(8,128)(2,1)} %query_projection.1.query_ref, bf16[32,32,512]{2,1,0:T(8,128)(2,1)} %get-tuple-element.28.refs_0_, bf16[32,32,512]{2,1,0:T(8,128)(2,1)} %get-tuple-element.29.refs_1_, bf16[32,32,512]{2,1,0:T(8,128)(2,1)} %get-tuple-element.30.refs_2_, ...), custom_call_target="tpu_custom_call" | custom-call | flops 4000000000 | bytes 12582912 | tf_op jit(solution)/shard_map/attend/pallas_call | solution.py:238
  196.0 10.6 %mix.1 = (bf16[128,2048]{1,0:T(8,128)(2,1)}, bf16[128,2048]{1,0:T(8,128)(2,1)}, bf16[128,2048]{1,0:T(8,128)(2,1)}, bf16[128,2048]{1,0:T(8,128)(2,1)}, bf16[128,2...) custom-call(s32[4]{0:T(128)} %and_select_fusion.8.turn_ref, ...), custom_call_target="tpu_custom_call" | custom-call | flops 4294967296 | bytes 14680064 | tf_op jit(solution)/shard_map/mix/pallas_call | solution.py:270
  206.9 2.5 %collective-permute-start.46 = (bf16[128,2048]{1,0:T(8,128)(2,1)}, bf16[128,2048]{1,0:T(8,128)(2,1)S(1)}, u32[]{:S(2)}, u32[]{:S(2)}) collective-permute-start(bf16[128,2048]{1,0:T(8,128)(2,1)} %get-tuple-element.44), channel_id=1, source_target_pairs={{0,6},{2,0},{4,2},{6,4},{1,7},{3,1},{5,3},{7,5},{8,14},{10,8},{12,... | collective-permute-start | bytes 1572872 | tf_op jit(solution)/shard_map/ppermute | solution.py:23
  210.9 10.4 %collective-permute-done.42 = bf16[128,2048]{1,0:T(8,128)(2,1)S(1)} collective-permute-done((bf16[128,2048]{1,0:T(8,128)(2,1)}, bf16[128,2048]{1,0:T(8,128)(2,1)S(1)}, u32[]{:S(2)}, u32[]{:S(2)}) %collective-permute-start.42) | collective-permute-done | bytes 524320 | tf_op jit(solution)/shard_map/ppermute | solution.py:23
  222.8 2.7 %collective-permute-start.47 = (bf16[128,2048]{1,0:T(8,128)(2,1)S(1)}, bf16[128,2048]{1,0:T(8,128)(2,1)S(1)}, u32[]{:S(2)}, u32[]{:S(2)}) collective-permute-start(bf16[128,2048]{1,0:T(8,128)(2,1)S(1)} %add_convert_fusion), channel_id=1, source_target_pairs={{0,6},{2,0},{4,2},{6,4},{1,7},{3,1},{5,3},{7,5},{8,14},{10,8},{12,... | collective-permute-start | bytes 1572872 | tf_op jit(solution)/shard_map/ppermute | solution.py:23
  225.5 6.3 %collective-permute-done.44.refs_2_ = bf16[128,2048]{1,0:T(8,128)(2,1)S(1)} collective-permute-done((bf16[128,2048]{1,0:T(8,128)(2,1)}, bf16[128,2048]{1,0:T(8,128)(2,1)S(1)}, u32[]{:S(2)}, u32[]{:S(2)}) %collective-permute-start.44) | collective-permute-done | bytes 524320 | tf_op jit(solution)/shard_map/ppermute | solution.py:23
  232.6 11.2 %collective-permute-done.43.refs_1_ = bf16[128,2048]{1,0:T(8,128)(2,1)S(1)} collective-permute-done((bf16[128,2048]{1,0:T(8,128)(2,1)S(1)}, bf16[128,2048]{1,0:T(8,128)(2,1)S(1)}, u32[]{:S(2)}, u32[]{:S(2)}) %collective-permute-start.43) | collective-permute-done | bytes 524320 | tf_op jit(solution)/shard_map/ppermute | solution.py:23
  244.8 3.9 %final.1 = bf16[128,4096]{1,0:T(8,128)(2,1)} custom-call(s32[16]{0:T(128)} %get-tuple-element.48.owner_ref, bf16[128,2048]{1,0:T(8,128)(2,1)} %get-tuple-element.37.refs_0_, bf16[128,2048]{1,0:T(8,128)(2,1)} %copy-done.12, bf16[128,2048]{1,0:T(8,128)(2,1)} %copy-done.10, bf16[128,2048]{1,0:T(8,128)(2,1)} %get-tuple-element.41.refs_3_, ...), custom_call_target="tpu_custom_call" | custom-call | tf_op jit(solution)/shard_map/final/pallas_call | solution.py:297
  (185 shorter events, 50.6 us)
Async XLA Ops:
  16.9 41.0 %collective-permute-start.13 = (bf16[4,8,16,896]{3,2,1,0:T(8,128)(2,1)S(1)}, bf16[4,8,16,896]{3,2,1,0:T(8,128)(2,1)S(1)}, u32[]{:S(2)}, u32[]{:S(2)}) collective-permute-start(bf16[4,8,16,896]{3,2,1,0:T(8,128)(2,1)S(1)} %pad_maximum_fusion.2), channel_id=1, source_target_pairs={{0,8},{8,16},{16,24},{24,0},{1,9},{9,17},{17,25},{25,1},{2,10},{10... | collective-permute-start | bytes 2752520 | tf_op jit(solution)/shard_map/ppermute | solution.py:23
  18.3 42.3 %collective-permute-start.14 = (bf16[4,8,16,896]{3,2,1,0:T(8,128)(2,1)S(1)}, bf16[4,8,16,896]{3,2,1,0:T(8,128)(2,1)S(1)}, u32[]{:S(2)}, u32[]{:S(2)}) collective-permute-start(bf16[4,8,16,896]{3,2,1,0:T(8,128)(2,1)S(1)} %pad_maximum_fusion.2), channel_id=1, source_target_pairs={{0,24},{8,0},{16,8},{24,16},{1,25},{9,1},{17,9},{25,17},{2,26},{10... | collective-permute-start | bytes 2752520 | tf_op jit(solution)/shard_map/ppermute | solution.py:23
  19.8 25.7 %collective-permute-start.2 = (bf16[256,512]{1,0:T(8,128)(2,1)S(1)}, bf16[256,512]{1,0:T(8,128)(2,1)}, u32[]{:S(2)}, u32[]{:S(2)}) collective-permute-start(bf16[256,512]{1,0:T(8,128)(2,1)S(1)} %copy-done.16), channel_id=1, source_target_pairs={{0,16},{8,24},{16,0},{24,8},{1,17},{9,25},{17,1},{25,9},{2,18},{10... | collective-permute-start | bytes 786440 | tf_op jit(solution)/shard_map/ppermute | solution.py:23
  21.4 28.5 %collective-permute-start.1 = (bf16[256,512]{1,0:T(8,128)(2,1)S(1)}, bf16[256,512]{1,0:T(8,128)(2,1)S(1)}, u32[]{:S(2)}, u32[]{:S(2)}) collective-permute-start(bf16[256,512]{1,0:T(8,128)(2,1)S(1)} %copy-done.16), channel_id=1, source_target_pairs={{0,24},{8,0},{16,8},{24,16},{1,25},{9,1},{17,9},{25,17},{2,26},{10... | collective-permute-start | bytes 786440 | tf_op jit(solution)/shard_map/ppermute | solution.py:23
  22.2 31.8 %collective-permute-start = (bf16[256,512]{1,0:T(8,128)(2,1)S(1)}, bf16[256,512]{1,0:T(8,128)(2,1)S(1)}, u32[]{:S(2)}, u32[]{:S(2)}) collective-permute-start(bf16[256,512]{1,0:T(8,128)(2,1)S(1)} %copy-done.16), channel_id=1, source_target_pairs={{0,8},{8,16},{16,24},{24,0},{1,9},{9,17},{17,25},{25,1},{2,10},{10... | collective-permute-start | bytes 786440 | tf_op jit(solution)/shard_map/ppermute | solution.py:23
  45.6 16.2 %collective-permute-start.8 = (bf16[512,256]{1,0:T(8,128)(2,1)S(1)}, bf16[512,256]{1,0:T(8,128)(2,1)S(1)}, u32[]{:S(2)}, u32[]{:S(2)}) collective-permute-start(bf16[512,256]{1,0:T(8,128)(2,1)S(1)} %copy-done.17), channel_id=1, source_target_pairs={{0,64},{32,96},{64,0},{96,32},{1,65},{33,97},{65,1},{97,33},{2,66}... | collective-permute-start | bytes 786440 | tf_op jit(solution)/shard_map/ppermute | solution.py:23
  67.1 34.3 %collective-permute-start.9 = (bf16[4,256,512]{2,1,0:T(8,128)(2,1)}, bf16[4,256,512]{2,1,0:T(8,128)(2,1)}, u32[]{:S(2)}, u32[]{:S(2)}) collective-permute-start(bf16[4,256,512]{2,1,0:T(8,128)(2,1)} %pad_maximum_fusion.refs_0_), channel_id=1, source_target_pairs={{0,32},{32,64},{64,96},{96,0},{1,33},{33,65},{65,97},{97,1},{2,34}... | collective-permute-start | bytes 3145736 | tf_op jit(solution)/shard_map/ppermute | solution.py:23
  68.5 31.3 %collective-permute-start.21 = (bf16[4,56,1024]{2,1,0:T(8,128)(2,1)S(1)}, bf16[4,56,1024]{2,1,0:T(8,128)(2,1)S(1)}, u32[]{:S(2)}, u32[]{:S(2)}) collective-permute-start(bf16[4,56,1024]{2,1,0:T(8,128)(2,1)S(1)} %pad_maximum_fusion.3.refs_0_), channel_id=1, source_target_pairs={{0,32},{32,64},{64,96},{96,0},{1,33},{33,65},{65,97},{97,1},{2,34}... | collective-permute-start | bytes 1376264 | tf_op jit(solution)/shard_map/ppermute | solution.py:23
  69.0 38.6 %collective-permute-start.10 = (bf16[4,256,512]{2,1,0:T(8,128)(2,1)}, bf16[4,256,512]{2,1,0:T(8,128)(2,1)}, u32[]{:S(2)}, u32[]{:S(2)}) collective-permute-start(bf16[4,256,512]{2,1,0:T(8,128)(2,1)} %pad_maximum_fusion.refs_0_), channel_id=1, source_target_pairs={{0,96},{32,0},{64,32},{96,64},{1,97},{33,1},{65,33},{97,65},{2,98}... | collective-permute-start | bytes 3145736 | tf_op jit(solution)/shard_map/ppermute | solution.py:23
  80.6 29.0 %collective-permute-start.25 = (bf16[32,16,896]{2,1,0:T(8,128)(2,1)}, bf16[32,16,896]{2,1,0:T(8,128)(2,1)}, u32[]{:S(2)}, u32[]{:S(2)}) collective-permute-start(bf16[32,16,896]{2,1,0:T(8,128)(2,1)} %pick.1.mine_ref), channel_id=1, source_target_pairs={{0,2},{2,4},{4,6},{6,0},{1,3},{3,5},{5,7},{7,1},{8,10},{10,12},{12... | collective-permute-start | bytes 2752520 | tf_op jit(solution)/shard_map/ppermute | solution.py:23
  81.9 33.6 %collective-permute-start.27 = (bf16[32,16,896]{2,1,0:T(8,128)(2,1)}, bf16[32,16,896]{2,1,0:T(8,128)(2,1)S(1)}, u32[]{:S(2)}, u32[]{:S(2)}) collective-permute-start(bf16[32,16,896]{2,1,0:T(8,128)(2,1)} %pick.1.mine_ref), channel_id=1, source_target_pairs={{0,6},{2,0},{4,2},{6,4},{1,7},{3,1},{5,3},{7,5},{8,14},{10,8},{12,... | collective-permute-start | bytes 2752520 | tf_op jit(solution)/shard_map/ppermute | solution.py:23
  107.6 19.4 %collective-permute-start.11 = (bf16[2,256,512]{2,1,0:T(8,128)(2,1)S(1)}, bf16[2,256,512]{2,1,0:T(8,128)(2,1)S(1)}, u32[]{:S(2)}, u32[]{:S(2)}) collective-permute-start(bf16[2,256,512]{2,1,0:T(8,128)(2,1)S(1)} %slice.40), channel_id=1, source_target_pairs={{0,32},{32,64},{64,96},{96,0},{1,33},{33,65},{65,97},{97,1},{2,34}... | collective-permute-start | bytes 1572872 | tf_op jit(solution)/shard_map/ppermute | solution.py:23
  107.6 31.5 %collective-permute-start.33 = (bf16[4,512,256]{2,1,0:T(8,128)(2,1)S(1)}, bf16[4,512,256]{2,1,0:T(8,128)(2,1)}, u32[]{:S(2)}, u32[]{:S(2)}) collective-permute-start(bf16[4,512,256]{2,1,0:T(8,128)(2,1)S(1)} %copy-done.6), channel_id=1, source_target_pairs={{0,8},{8,16},{16,24},{24,0},{1,9},{9,17},{17,25},{25,1},{2,10},{10... | collective-permute-start | bytes 3145736 | tf_op jit(solution)/shard_map/ppermute | solution.py:23
  109.6 17.4 %collective-permute-start.12 = (bf16[2,256,512]{2,1,0:T(8,128)(2,1)S(1)}, bf16[2,256,512]{2,1,0:T(8,128)(2,1)S(1)}, u32[]{:S(2)}, u32[]{:S(2)}) collective-permute-start(bf16[2,256,512]{2,1,0:T(8,128)(2,1)S(1)} %slice.41), channel_id=1, source_target_pairs={{0,96},{32,0},{64,32},{96,64},{1,97},{33,1},{65,33},{97,65},{2,98}... | collective-permute-start | bytes 1572872 | tf_op jit(solution)/shard_map/ppermute | solution.py:23
  114.1 19.9 %collective-permute-start.29 = (bf16[16,16,896]{2,1,0:T(8,128)(2,1)S(1)}, bf16[16,16,896]{2,1,0:T(8,128)(2,1)S(1)}, u32[]{:S(2)}, u32[]{:S(2)}) collective-permute-start(bf16[16,16,896]{2,1,0:T(8,128)(2,1)S(1)} %slice.46), channel_id=1, source_target_pairs={{0,2},{2,4},{4,6},{6,0},{1,3},{3,5},{5,7},{7,1},{8,10},{10,12},{12... | collective-permute-start | bytes 1376264 | tf_op jit(solution)/shard_map/ppermute | solution.py:23
  127.0 25.0 %collective-permute-start.34 = (bf16[4,512,256]{2,1,0:T(8,128)(2,1)S(1)}, bf16[4,512,256]{2,1,0:T(8,128)(2,1)}, u32[]{:S(2)}, u32[]{:S(2)}) collective-permute-start(bf16[4,512,256]{2,1,0:T(8,128)(2,1)S(1)} %copy-done.6), channel_id=1, source_target_pairs={{0,24},{8,0},{16,8},{24,16},{1,25},{9,1},{17,9},{25,17},{2,26},{10... | collective-permute-start | bytes 3145736 | tf_op jit(solution)/shard_map/ppermute | solution.py:23
  127.1 26.7 %collective-permute-start.17 = (bf16[32,16,896]{2,1,0:T(8,128)(2,1)}, bf16[32,16,896]{2,1,0:T(8,128)(2,1)}, u32[]{:S(2)}, u32[]{:S(2)}) collective-permute-start(bf16[32,16,896]{2,1,0:T(8,128)(2,1)} %pick.1.mine_ref), channel_id=1, source_target_pairs={{0,1},{1,0},{2,3},{3,2},{4,5},{5,4},{6,7},{7,6},{8,9},{9,8},{10,11... | collective-permute-start | bytes 2752520 | tf_op jit(solution)/shard_map/ppermute | solution.py:23
  134.1 20.3 %collective-permute-start.26 = (bf16[32,16,896]{2,1,0:T(8,128)(2,1)}, bf16[32,16,896]{2,1,0:T(8,128)(2,1)}, u32[]{:S(2)}, u32[]{:S(2)}) collective-permute-start(bf16[32,16,896]{2,1,0:T(8,128)(2,1)} %collective-permute-done.25.mine_ref), channel_id=1, source_target_pairs={{0,1},{1,0},{2,3},{3,2},{4,5},{5,4},{6,7},{7,6},{8,9},{9,8},{10,11... | collective-permute-start | bytes 2752520 | tf_op jit(solution)/shard_map/ppermute | solution.py:23
  138.9 29.3 %collective-permute-start.28 = (bf16[32,16,896]{2,1,0:T(8,128)(2,1)}, bf16[32,16,896]{2,1,0:T(8,128)(2,1)S(1)}, u32[]{:S(2)}, u32[]{:S(2)}) collective-permute-start(bf16[32,16,896]{2,1,0:T(8,128)(2,1)} %copy-done.20), channel_id=1, source_target_pairs={{0,1},{1,0},{2,3},{3,2},{4,5},{5,4},{6,7},{7,6},{8,9},{9,8},{10,11... | collective-permute-start | bytes 2752520 | tf_op jit(solution)/shard_map/ppermute | solution.py:23
  139.1 36.6 %collective-permute-start.31 = (bf16[32,16,896]{2,1,0:T(8,128)(2,1)S(1)}, bf16[32,16,896]{2,1,0:T(8,128)(2,1)S(1)}, u32[]{:S(2)}, u32[]{:S(2)}) collective-permute-start(bf16[32,16,896]{2,1,0:T(8,128)(2,1)S(1)} %constant_dynamic-update-slice_fusion.2.mine_ref), channel_id=1, source_target_pairs={{0,1},{1,0},{2,3},{3,2},{4,5},{5,4},{6,7},{7,6},{8,9},{9,8},{10,11... | collective-permute-start | bytes 2752520 | tf_op jit(solution)/shard_map/ppermute | solution.py:23
  152.1 41.2 %collective-permute-start.37 = (bf16[4,512,256]{2,1,0:T(8,128)(2,1)S(1)}, bf16[4,512,256]{2,1,0:T(8,128)(2,1)S(1)}, u32[]{:S(2)}, u32[]{:S(2)}) collective-permute-start(bf16[4,512,256]{2,1,0:T(8,128)(2,1)S(1)} %copy-done.6), channel_id=1, source_target_pairs={{0,1},{1,0},{2,3},{3,2},{4,5},{5,4},{6,7},{7,6},{8,9},{9,8},{10,11... | collective-permute-start | bytes 3145736 | tf_op jit(solution)/shard_map/ppermute | solution.py:23
  153.8 21.2 %collective-permute-start.35 = (bf16[2,512,256]{2,1,0:T(8,128)(2,1)S(1)}, bf16[2,512,256]{2,1,0:T(8,128)(2,1)S(1)}, u32[]{:S(2)}, u32[]{:S(2)}) collective-permute-start(bf16[2,512,256]{2,1,0:T(8,128)(2,1)S(1)} %slice.48), channel_id=1, source_target_pairs={{0,8},{8,16},{16,24},{24,0},{1,9},{9,17},{17,25},{25,1},{2,10},{10... | collective-permute-start | bytes 1572872 | tf_op jit(solution)/shard_map/ppermute | solution.py:23
  154.4 21.2 %collective-permute-start.36 = (bf16[2,512,256]{2,1,0:T(8,128)(2,1)S(1)}, bf16[2,512,256]{2,1,0:T(8,128)(2,1)}, u32[]{:S(2)}, u32[]{:S(2)}) collective-permute-start(bf16[2,512,256]{2,1,0:T(8,128)(2,1)S(1)} %slice.49), channel_id=1, source_target_pairs={{0,24},{8,0},{16,8},{24,16},{1,25},{9,1},{17,9},{25,17},{2,26},{10... | collective-permute-start | bytes 1572872 | tf_op jit(solution)/shard_map/ppermute | solution.py:23
  168.2 26.0 %collective-permute-start.38 = (bf16[4,512,256]{2,1,0:T(8,128)(2,1)}, bf16[4,512,256]{2,1,0:T(8,128)(2,1)S(1)}, u32[]{:S(2)}, u32[]{:S(2)}) collective-permute-start(bf16[4,512,256]{2,1,0:T(8,128)(2,1)} %collective-permute-done.33.refs_1_), channel_id=1, source_target_pairs={{0,1},{1,0},{2,3},{3,2},{4,5},{5,4},{6,7},{7,6},{8,9},{9,8},{10,11... | collective-permute-start | bytes 3145736 | tf_op jit(solution)/shard_map/ppermute | solution.py:23
  175.0 19.2 %collective-permute-start.39 = (bf16[4,512,256]{2,1,0:T(8,128)(2,1)}, bf16[4,512,256]{2,1,0:T(8,128)(2,1)S(1)}, u32[]{:S(2)}, u32[]{:S(2)}) collective-permute-start(bf16[4,512,256]{2,1,0:T(8,128)(2,1)} %collective-permute-done.34.refs_2_), channel_id=1, source_target_pairs={{0,1},{1,0},{2,3},{3,2},{4,5},{5,4},{6,7},{7,6},{8,9},{9,8},{10,11... | collective-permute-start | bytes 3145736 | tf_op jit(solution)/shard_map/ppermute | solution.py:23
  175.7 18.6 %collective-permute-start.40 = (bf16[2,512,256]{2,1,0:T(8,128)(2,1)S(1)}, bf16[2,512,256]{2,1,0:T(8,128)(2,1)S(1)}, u32[]{:S(2)}, u32[]{:S(2)}) collective-permute-start(bf16[2,512,256]{2,1,0:T(8,128)(2,1)S(1)} %collective-permute-done.35.refs_3_), channel_id=1, source_target_pairs={{0,1},{1,0},{2,3},{3,2},{4,5},{5,4},{6,7},{7,6},{8,9},{9,8},{10,11... | collective-permute-start | bytes 1572872 | tf_op jit(solution)/shard_map/ppermute | solution.py:23
  175.8 18.5 %collective-permute-start.41 = (bf16[2,512,256]{2,1,0:T(8,128)(2,1)}, bf16[2,512,256]{2,1,0:T(8,128)(2,1)S(1)}, u32[]{:S(2)}, u32[]{:S(2)}) collective-permute-start(bf16[2,512,256]{2,1,0:T(8,128)(2,1)} %collective-permute-done.36.refs_4_), channel_id=1, source_target_pairs={{0,1},{1,0},{2,3},{3,2},{4,5},{5,4},{6,7},{7,6},{8,9},{9,8},{10,11... | collective-permute-start | bytes 1572872 | tf_op jit(solution)/shard_map/ppermute | solution.py:23
  206.9 15.7 %collective-permute-start.46 = (bf16[128,2048]{1,0:T(8,128)(2,1)}, bf16[128,2048]{1,0:T(8,128)(2,1)S(1)}, u32[]{:S(2)}, u32[]{:S(2)}) collective-permute-start(bf16[128,2048]{1,0:T(8,128)(2,1)} %get-tuple-element.44), channel_id=1, source_target_pairs={{0,6},{2,0},{4,2},{6,4},{1,7},{3,1},{5,3},{7,5},{8,14},{10,8},{12,... | collective-permute-start | bytes 1572872 | tf_op jit(solution)/shard_map/ppermute | solution.py:23
  209.5 22.3 %collective-permute-start.44 = (bf16[128,2048]{1,0:T(8,128)(2,1)}, bf16[128,2048]{1,0:T(8,128)(2,1)S(1)}, u32[]{:S(2)}, u32[]{:S(2)}) collective-permute-start(bf16[128,2048]{1,0:T(8,128)(2,1)} %get-tuple-element.40), channel_id=1, source_target_pairs={{0,6},{2,0},{4,2},{6,4},{1,7},{3,1},{5,3},{7,5},{8,14},{10,8},{12,... | collective-permute-start | bytes 1572872 | tf_op jit(solution)/shard_map/ppermute | solution.py:23
  210.8 21.7 %collective-permute-start.45 = (bf16[128,2048]{1,0:T(8,128)(2,1)}, bf16[128,2048]{1,0:T(8,128)(2,1)S(1)}, u32[]{:S(2)}, u32[]{:S(2)}) collective-permute-start(bf16[128,2048]{1,0:T(8,128)(2,1)} %get-tuple-element.42), channel_id=1, source_target_pairs={{0,2},{2,4},{4,6},{6,0},{1,3},{3,5},{5,7},{7,1},{8,10},{10,12},{12... | collective-permute-start | bytes 1572872 | tf_op jit(solution)/shard_map/ppermute | solution.py:23
  222.5 21.3 %collective-permute-start.43 = (bf16[128,2048]{1,0:T(8,128)(2,1)S(1)}, bf16[128,2048]{1,0:T(8,128)(2,1)S(1)}, u32[]{:S(2)}, u32[]{:S(2)}) collective-permute-start(bf16[128,2048]{1,0:T(8,128)(2,1)S(1)} %add_convert_fusion.1), channel_id=1, source_target_pairs={{0,2},{2,4},{4,6},{6,0},{1,3},{3,5},{5,7},{7,1},{8,10},{10,12},{12... | collective-permute-start | bytes 1572872 | tf_op jit(solution)/shard_map/ppermute | solution.py:23
  222.8 21.1 %collective-permute-start.47 = (bf16[128,2048]{1,0:T(8,128)(2,1)S(1)}, bf16[128,2048]{1,0:T(8,128)(2,1)S(1)}, u32[]{:S(2)}, u32[]{:S(2)}) collective-permute-start(bf16[128,2048]{1,0:T(8,128)(2,1)S(1)} %add_convert_fusion), channel_id=1, source_target_pairs={{0,6},{2,0},{4,2},{6,4},{1,7},{3,1},{5,3},{7,5},{8,14},{10,8},{12,... | collective-permute-start | bytes 1572872 | tf_op jit(solution)/shard_map/ppermute | solution.py:23
  (57 other events, 800.1 us)

commit v2 on v1

v2 whole, which is shorter than its diff:
```python
import functools
import math

import jax
import jax.numpy as jnp
from jax import lax
from jax.experimental import pallas as pl
from jax.experimental.pallas import tpu as pltpu
from jax.sharding import PartitionSpec as P

HEAD = 128
EPS = 1e-06
RING = 4
ORDER = (0, 3, 1, 2)
PLACE = (0, 2, 3, 1)
MIB = 1024 * 1024
ANY = pl.BlockSpec(memory_space=pl.ANY)
VMEM = pl.BlockSpec(memory_space=pltpu.VMEM)


def shift(value, axis, step):
    size = lax.axis_size(axis)
    return lax.ppermute(value, axis, [(i, (i + step) % size) for i in range(size)])


def hold(values, *earlier):
    count = len(values)
    return list(lax.optimization_barrier(tuple(values) + earlier)[:count])


def line(block, axis):
    return [block, shift(block, axis, 1), shift(block, axis, -1), shift(block, axis, 2)]


def ring_near(blocks, axis):
    return [blocks, shift(blocks, axis, 1), shift(blocks, axis, -1)]


def after(value, *earlier):
    return hold([value], *earlier)[0]


def far_halves(pieces):
    _, before, behind = pieces
    half = before.shape[0] // 2
    return [before[:half], behind[half:]]


def ring_far(pieces, halves, axis):
    return pieces + [shift(halves[0], axis, 1), shift(halves[1], axis, -1)]


BLOCKS = tuple((p, s) for p in range(3) for s in range(4)) + ((3, 0), (3, 1), (4, 0), (4, 1))


def block_owners(z, y):
    major = jnp.array([ORDER[k // 4] for k in range(16)], jnp.int32)
    minor = jnp.array([ORDER[k % 4] for k in range(16)], jnp.int32)
    by_zy = ((z + minor) % RING) * RING + (y + major) % RING
    by_yz = ((z + major) % RING) * RING + (y + minor) % RING
    return by_zy.astype(jnp.int32), by_yz.astype(jnp.int32)


def pick_kernel(place_ref, *refs):
    pieces, (out_ref, sem) = refs[:10], refs[10:]
    bounds = (0, 16, 32, 48, 56, 64, 80, 96, 112, 120, 128)

    def one(j, carry):
        place = place_ref[j]
        for low, high, piece in zip(bounds[:-1], bounds[1:], pieces):

            @pl.when((place >= low) & (place < high))
            def _():
                pltpu.make_async_copy(piece.at[place - low], out_ref.at[j], sem).start()

        return carry

    lax.fori_loop(0, out_ref.shape[0], one, 0)
    pltpu.make_async_copy(out_ref, out_ref, sem).wait()


def pick(place, pieces, count):
    shape = pieces[0].shape[1:]
    return pl.pallas_call(
        pick_kernel,
        out_shape=jax.ShapeDtypeStruct((count,) + shape, jnp.bfloat16),
        grid_spec=pltpu.PrefetchScalarGridSpec(
            num_scalar_prefetch=1,
            grid=(1,),
            in_specs=[ANY] * 10,
            out_specs=VMEM,
            scratch_shapes=[pltpu.SemaphoreType.DMA],
        ),
        compiler_params=pltpu.CompilerParams(vmem_limit_bytes=8 * MIB),
        cost_estimate=pl.CostEstimate(flops=0, bytes_accessed=2 * MIB, transcendentals=0),
        name="pick",
    )(place, *pieces)


def arrange_kernel(owner_ref, *refs):
    pieces, (out_ref, sem) = refs[:5], refs[5:]
    for k, (p, s) in enumerate(BLOCKS):
        pltpu.make_async_copy(pieces[p].at[s], out_ref.at[owner_ref[k]], sem).start()
    pltpu.make_async_copy(out_ref, out_ref, sem).wait()


def arrange(owners, pieces):
    return pl.pallas_call(
        arrange_kernel,
        out_shape=jax.ShapeDtypeStruct((16,) + pieces[0].shape[1:], jnp.bfloat16),
        grid_spec=pltpu.PrefetchScalarGridSpec(
            num_scalar_prefetch=1,
            grid=(1,),
            in_specs=[ANY] * 5,
            out_specs=VMEM,
            scratch_shapes=[pltpu.SemaphoreType.DMA],
        ),
        compiler_params=pltpu.CompilerParams(vmem_limit_bytes=8 * MIB),
        cost_estimate=pl.CostEstimate(flops=0, bytes_accessed=4 * MIB, transcendentals=0),
        name="arrange",
    )(owners, *pieces)


def normed(field):
    parts = []
    for h in range(field.shape[1] // HEAD):
        part = field[:, h * HEAD : (h + 1) * HEAD]
        scale = lax.rsqrt(jnp.mean(part * part, axis=-1, keepdims=True) + EPS)
        parts.append((part * scale).astype(jnp.bfloat16))
    return parts


def query_kernel(owner_ref, tokens_ref, *refs):
    pieces, (out_ref, weight_ref, sem) = refs[:5], refs[5:]

    @pl.when(pl.program_id(0) == 0)
    def _():
        for k, (p, s) in enumerate(BLOCKS):
            rows = pl.multiple_of(owner_ref[k] * 256, 256)
            pltpu.make_async_copy(
                pieces[p].at[s], weight_ref.at[pl.ds(rows, 256), :], sem
            ).start()
        pltpu.make_async_copy(weight_ref, weight_ref, sem).wait()

    field = jnp.dot(tokens_ref[...], weight_ref[...], preferred_element_type=jnp.float32)
    for h, part in enumerate(normed(field)):
        out_ref[:, h * HEAD : (h + 1) * HEAD] = part


def query_projection(owners, tokens, pieces):
    rows, depth = tokens.shape
    width = pieces[0].shape[2]
    block = 256
    return pl.pallas_call(
        query_kernel,
        out_shape=jax.ShapeDtypeStruct((rows, width), jnp.bfloat16),
        grid_spec=pltpu.PrefetchScalarGridSpec(
            num_scalar_prefetch=1,
            grid=(rows // block,),
            in_specs=[pl.BlockSpec((block, depth), lambda i, s: (i, 0))] + [ANY] * 5,
            out_specs=pl.BlockSpec((block, width), lambda i, s: (i, 0)),
            scratch_shapes=[
                pltpu.VMEM((depth, width), jnp.bfloat16),
                pltpu.SemaphoreType.DMA,
            ],
        ),
        compiler_params=pltpu.CompilerParams(vmem_limit_bytes=20 * MIB),
        cost_estimate=pl.CostEstimate(
            flops=2 * rows * depth * width, bytes_accessed=14 * MIB, transcendentals=0
        ),
        name="query_projection",
    )(owners, tokens, *pieces)


def attend_kernel(block_ref, query_ref, panel_ref, *refs):
    row_refs, out_ref = refs[:10], refs[10]
    block = block_ref[pl.program_id(0)]
    half = panel_ref.shape[1] // 2
    heads = half // HEAD
    near, share, depth = row_refs[0].shape
    low, high = row_refs[3:5], row_refs[8:10]
    shares = [r[...] for r in row_refs[:3] + row_refs[5:8]]
    shares += [jnp.where(block < 4, pair[0][...], pair[1][...]) for pair in (low, high)]
    rows = jnp.concatenate(shares, axis=1).reshape(near * 8 * share, depth)
    keys = normed(jnp.dot(rows, panel_ref[:, :half], preferred_element_type=jnp.float32))
    values = jnp.dot(rows, panel_ref[:, half:], preferred_element_type=jnp.float32).astype(
        jnp.bfloat16
    )
    span, per = 64, near * 4 * share
    scale = math.log2(math.e) / math.sqrt(HEAD)
    pairs = [(s, h) for s in range(2) for h in range(heads)]
    scores = [
        lax.dot_general(
            query_ref[s * span : (s + 1) * span, h * HEAD : (h + 1) * HEAD],
            keys[h][s * per : (s + 1) * per],
            (((1,), (1,)), ((), ())),
            preferred_element_type=jnp.float32,
        )
        for s, h in pairs
    ]
    raised = [jnp.exp2(score * scale) for score in scores]
    sums = [jnp.sum(r, axis=-1, keepdims=True) for r in raised]
    for (s, h), r, total in zip(pairs, raised, sums):
        lanes = slice(h * HEAD, (h + 1) * HEAD)
        mixed = jnp.dot(
            r.astype(jnp.bfloat16),
            values[s * per : (s + 1) * per, lanes],
            preferred_element_type=jnp.float32,
        )
        out_ref[s * span : (s + 1) * span, lanes] = (mixed / total).astype(jnp.bfloat16)


def attend(blocks, query, panel, pieces):
    width = query.shape[1]
    count, block, near = blocks.shape[0], 128, 4
    shape = (near,) + pieces[0].shape[1:]
    spec = pl.BlockSpec(shape, lambda i, b: (b[i], 0, 0))
    low = pl.BlockSpec(shape, lambda i, b: (jnp.minimum(b[i], 3), 0, 0))
    high = pl.BlockSpec(shape, lambda i, b: (jnp.maximum(b[i] - 4, 0), 0, 0))
    return pl.pallas_call(
        attend_kernel,
        out_shape=jax.ShapeDtypeStruct((count * block, width), jnp.bfloat16),
        grid_spec=pltpu.PrefetchScalarGridSpec(
            num_scalar_prefetch=1,
            grid=(count,),
            in_specs=[pl.BlockSpec((block, width), lambda i, b: (b[i], 0)), VMEM]
            + [spec, spec, spec, low, high] * 2,
            out_specs=pl.BlockSpec((block, width), lambda i, b: (i, 0)),
        ),
        compiler_params=pltpu.CompilerParams(vmem_limit_bytes=24 * MIB),
        cost_estimate=pl.CostEstimate(
            flops=6_000_000_000, bytes_accessed=12 * MIB, transcendentals=2_000_000
        ),
        name="attend",
    )(blocks, query, panel, *pieces)


def mix_kernel(mine_ref, other_ref, *refs):
    mine_w, other_w, outs = refs[:5], refs[5:10], refs[10:]
    rows = mine_ref.shape[0] // 4
    for j, (p, s) in enumerate(BLOCKS):
        total = jnp.dot(mine_ref[...], mine_w[p][s], preferred_element_type=jnp.float32)
        total += jnp.dot(other_ref[...], other_w[p][s], preferred_element_type=jnp.float32)
        total = total.astype(jnp.bfloat16)
        at = j % 8 * 256
        for k in range(4):
            outs[k * 2 + j // 8][:, at : at + 256] = total[k * rows : (k + 1) * rows]


def mix(mine, other, mine_w, other_w):
    shape = jax.ShapeDtypeStruct((128, 2048), jnp.bfloat16)
    return pl.pallas_call(
        mix_kernel,
        out_shape=[shape] * 8,
        in_specs=[VMEM] * 12,
        out_specs=[VMEM] * 8,
        compiler_params=pltpu.CompilerParams(vmem_limit_bytes=24 * MIB),
        cost_estimate=pl.CostEstimate(
            flops=2 * 512 * 1024 * 4096, bytes_accessed=14 * MIB, transcendentals=0
        ),
        name="mix",
    )(mine, other, *mine_w, *other_w)


def final_kernel(owner_ref, *refs):
    ins, out_ref = refs[:6], refs[6]
    for j in range(16):
        lanes = slice(j % 8 * 256, (j % 8 + 1) * 256)
        total = sum(ins[j // 8 * 3 + i][:, lanes].astype(jnp.float32) for i in range(3))
        at = pl.multiple_of(owner_ref[j] * 256, 256)
        out_ref[:, pl.ds(at, 256)] = total.astype(jnp.bfloat16)


def final(owners, parts):
    return pl.pallas_call(
        final_kernel,
        out_shape=jax.ShapeDtypeStruct((128, 4096), jnp.bfloat16),
        grid_spec=pltpu.PrefetchScalarGridSpec(
            num_scalar_prefetch=1, grid=(1,), in_specs=[VMEM] * 6, out_specs=VMEM
        ),
        compiler_params=pltpu.CompilerParams(vmem_limit_bytes=20 * MIB),
        name="final",
    )(owners, *parts)


def added(a, b):
    return (a.astype(jnp.float32) + b.astype(jnp.float32)).astype(jnp.bfloat16)


def local(tokens, database, neighbour_ids, shard_map, q_weight, k_weight, v_weight, o_weight):
    z, y, x, core = (lax.axis_index(a) for a in ("z", "y", "x", "core"))
    by_zy, by_yz = block_owners(z, y)
    stored = database.shape[0]

    ids = neighbour_ids.reshape(-1)
    span_ids = jnp.arange(shard_map.shape[0], dtype=jnp.int32)
    at = jnp.sum(jnp.where(ids[:, None] == span_ids[None, :], shard_map[None, :], 0), axis=1)
    owner, index = at // stored, at % stored
    dz, dy = (owner // RING - z) % RING, (owner % RING - y) % RING
    place_of = lambda d: jnp.where(d == 0, 0, jnp.where(d == 3, 1, d + 1))
    second = index // RING
    place = 64 * second + index % RING
    place += jnp.where(
        second == 0,
        place_of(dy) * 16 + place_of(dz) * RING,
        place_of(dz) * 16 + place_of(dy) * RING,
    )
    place = place.astype(jnp.int32)

    share = lax.dynamic_slice_in_dim(database, (x * 2 + core) * 16, 16, axis=1)
    first_z, second_y = line(share[:RING], "z"), line(share[RING:], "y")
    first_all, second_all = hold([jnp.stack(first_z), jnp.stack(second_y)])
    first_near, second_near = ring_near(first_all, "y"), ring_near(second_all, "z")
    halves = hold(far_halves(first_near) + far_halves(second_near))
    first_far = ring_far(first_near, halves[:2], "y")
    second_far = ring_far(second_near, halves[2:], "z")

    kv_weight = jnp.concatenate([k_weight, v_weight], axis=1)
    q_weight, o_weight, kv_weight = hold([q_weight, o_weight, kv_weight], *halves)
    lines = line(q_weight, "y") + line(o_weight, "z") + line(kv_weight, "z")

    flat = [p.reshape((-1,) + p.shape[2:]) for p in first_far + second_far]
    wanted = pick(place, flat, ids.shape[0])
    near_x = ring_near(wanted, "x")
    lines = hold(lines, wanted)
    q_all, o_all, kv_all = (jnp.stack(lines[i : i + RING]) for i in (0, RING, 2 * RING))
    q_near, kv_near = ring_near(q_all, "z"), ring_near(kv_all, "y")
    halves = hold(far_halves(kv_near))
    kv_far = ring_far(kv_near, halves, "y")
    o_near = ring_near(hold([o_all], *halves)[0], "y")
    blocks = arrange(by_zy, kv_far)
    panel = blocks.reshape(-1, blocks.shape[-1])

    halves = hold(far_halves(near_x) + far_halves(q_near), panel)
    pieces = hold(ring_far(near_x, halves[:2], "x"), *halves)
    q_far = ring_far(q_near, halves[2:], "z")
    query = query_projection(by_yz, tokens, q_far)
    halves = hold(far_halves(o_near), query)
    o_all = ring_far(o_near, halves, "y")
    pieces = pieces[:3] + hold(pieces[3:], *halves)
    pieces += [shift(p, "core", 1) for p in pieces]
    chips = (x + jnp.array([2, 1, 3, 0], jnp.int32)) % RING
    give = attend((chips * 2 + 1 - core).astype(jnp.int32), query, panel, pieces)
    other = shift(give, "core", 1)
    o_other = [shift(w, "core", 1) for w in hold(o_all[:3], give)]
    mine = attend((chips * 2 + core).astype(jnp.int32), after(query, give), panel, pieces)
    o_other += [shift(w, "core", 1) for w in hold(o_all[3:], mine)]
    t2a, t2b, t1a, t1b, t3a, t3b, t0a, t0b = mix(mine, other, o_all, o_other)

    to_next, to_last = shift(t2a, "x", 1), shift(t2b, "x", -1)
    r1b, r3a = shift(t1b, "x", 1), shift(t3a, "x", -1)
    r1a = shift(added(t1a, to_next), "x", 1)
    r3b = shift(added(t3b, to_last), "x", -1)
    return final(by_zy, [t0a, r1a, r3a, t0b, r1b, r3b])


def solution(mesh):
    grid = jax.sharding.Mesh(mesh.devices.reshape(4, 4, 4, 2), ("z", "y", "x", "core"))
    fsdp, grp = ("z", "y"), ("x", "core")
    in_specs = (
        P(fsdp, None),
        P(fsdp, None, None),
        P(fsdp, None),
        P(),
        P(fsdp, grp),
        P(fsdp, grp),
        P(fsdp, grp),
        P(grp, fsdp),
    )
    out_specs = P(fsdp + grp, None)
    return jax.shard_map(local, mesh=grid, in_specs=in_specs, out_specs=out_specs, check_vma=False)
```

time: 250 us -> 198 us (0.79)
  Pallas kernels: 64.1 us -> 33.6 us
  waiting for transfers between devices: 95 us -> 87 us
  local copies, waits for them, and re-layouts: 15 us -> 8.06 us
  other arithmetic: 8.68 us -> 5.09 us
    pallas_call x6 -> x3, Pallas kernels: 42.5 us -> 18.3 us  [the longest x2 13.8 us: attend(): pl.pallas_call(attend_kernel, out_shape=jax.ShapeDtypeStruct((count * blo...]
    ppermute x48 -> x56, waiting for transfers between devices: 95 us -> 87 us  [shift(): lax.ppermute(value, axis, [(i, (i + step) % size) for i in range(size)])]
    pallas_call x1, Pallas kernels: 11.3 us -> 6.71 us  [query_projection(): pl.pallas_call(query_kernel, out_shape=jax.ShapeDtypeStruct((rows, width)...]
    unnamed x85 -> x29, local copies, waits for them, and re-layouts: 6.55 us -> 2.68 us
    another operation x4 -> x5, other arithmetic: 5.47 us -> 2.76 us  [the longest x3 2.62 us: local(): jnp.stack(lines[i:i + RING])]
    slice x10 -> x13, local copies, waits for them, and re-layouts: 5.5 us -> 4.06 us  [the longest x12 3.07 us: far_halves(): return [before[:half], behind[half:]]]
    ppermute x48 -> x56, starting transfers between devices: 65.3 us -> 64 us  [shift(): lax.ppermute(value, axis, [(i, (i + step) % size) for i in range(size)])]
  transfers between devices with their start and end apart: 48 -> 56, of which waited for: 13 -> 27; matrix products, arithmetic and copies ran while one was open for 7% -> 5% of each run, Pallas kernels for 20% -> 14%
where the time goes in v2:
time: 198 us
  waiting for transfers between devices  87 us (44%)
  starting transfers between devices  64 us (32%)
  Pallas kernels  33.6 us (17%)
  local copies, waits for them, and re-layouts  8.06 us (4%)
  other arithmetic  5.09 us (3%)
    ppermute x56, waiting for transfers between devices, shift(): lax.ppermute(value, axis, [(i, (i + step) % size) for i in range(size)])  87 us
    ppermute x56, starting transfers between devices, shift(): lax.ppermute(value, axis, [(i, (i + step) % size) for i in range(size)])  64 us
    pallas_call x2, Pallas kernels, attend(): pl.pallas_call(attend_kernel, out_shape=jax.ShapeDtypeStruct((count * blo...  13.8 us
    pallas_call x1, Pallas kernels, query_projection(): pl.pallas_call(query_kernel, out_shape=jax.ShapeDtypeStruct((rows, width)...  6.71 us
    pallas_call x1, Pallas kernels, mix(): pl.pallas_call(mix_kernel, out_shape=[shape] * 8, in_specs=[VMEM] * 12, o...  4.51 us
  transfers between devices with their start and end apart: 56, of which 27 were waited for; matrix products, arithmetic and copies ran while one was open for 5% of the time, Pallas kernels for 14%

profile of v2, /device:TPU:1, one launch (start us, length us, event | category | flops | bytes accessed | tf_op | source)
XLA Modules:
  0.0 198.2 jit_solution(12621348632391103977)
XLA Ops:
  1.0 3.8 %collective-permute-start.5 = (bf16[4,16,896]{2,1,0:T(8,128)(2,1)S(1)}, bf16[4,16,896]{2,1,0:T(8,128)(2,1)S(1)}, u32[]{:S(2)}, u32[]{:S(2)}) collective-permute-start(bf16[4,16,896]{2,1,0:T(8,128)(2,1)S(1)} %get-tuple-element.109), channel_id=1, source_target_pairs={{0,16},{8,24},{16,0},{24,8},{1,17},{9,25},{17,1},{25,9},{2,18},{10... | collective-permute-start | bytes 344072 | tf_op jit(solution)/shard_map/ppermute | solution.py:23
  6.3 3.6 %collective-permute-start.2 = (bf16[4,16,896]{2,1,0:T(8,128)(2,1)S(1)}, bf16[4,16,896]{2,1,0:T(8,128)(2,1)S(1)}, u32[]{:S(2)}, u32[]{:S(2)}) collective-permute-start(bf16[4,16,896]{2,1,0:T(8,128)(2,1)S(1)} %get-tuple-element.110), channel_id=1, source_target_pairs={{0,64},{32,96},{64,0},{96,32},{1,65},{33,97},{65,1},{97,33},{2,66}... | collective-permute-start | bytes 344072 | tf_op jit(solution)/shard_map/ppermute | solution.py:23
  12.1 2.5 %collective-permute-done.1 = bf16[4,16,896]{2,1,0:T(8,128)(2,1)S(1)} collective-permute-done((bf16[4,16,896]{2,1,0:T(8,128)(2,1)S(1)}, bf16[4,16,896]{2,1,0:T(8,128)(2,1)S(1)}, u32[]{:S(2)}, u32[]{:S(2)}) %collective-permute-start.1) | collective-permute-done | bytes 114720 | tf_op jit(solution)/shard_map/ppermute | solution.py:23
  17.3 3.0 %collective-permute-start.9 = (bf16[4,4,16,896]{3,2,1,0:T(8,128)(2,1)S(1)}, bf16[4,4,16,896]{3,2,1,0:T(8,128)(2,1)S(1)}, u32[]{:S(2)}, u32[]{:S(2)}) collective-permute-start(bf16[4,4,16,896]{3,2,1,0:T(8,128)(2,1)S(1)} %pad_maximum_fusion.3), channel_id=1, source_target_pairs={{0,96},{32,0},{64,32},{96,64},{1,97},{33,1},{65,33},{97,65},{2,98}... | collective-permute-start | bytes 1376264 | tf_op jit(solution)/shard_map/ppermute | solution.py:23
  20.3 4.0 %collective-permute-done.7 = bf16[4,4,16,896]{3,2,1,0:T(8,128)(2,1)S(1)} collective-permute-done((bf16[4,4,16,896]{3,2,1,0:T(8,128)(2,1)S(1)}, bf16[4,4,16,896]{3,2,1,0:T(8,128)(2,1)S(1)}, u32[]{:S(2)}, u32[]{:S(2)}) %collective-permute-start.7) | collective-permute-done | bytes 458784 | tf_op jit(solution)/shard_map/ppermute | solution.py:23
  29.1 2.4 %collective-permute-done.8 = bf16[4,4,16,896]{3,2,1,0:T(8,128)(2,1)S(1)} collective-permute-done((bf16[4,4,16,896]{3,2,1,0:T(8,128)(2,1)S(1)}, bf16[4,4,16,896]{3,2,1,0:T(8,128)(2,1)S(1)}, u32[]{:S(2)}, u32[]{:S(2)}) %collective-permute-start.8) | collective-permute-done | bytes 458784 | tf_op jit(solution)/shard_map/ppermute | solution.py:23
  34.7 2.1 %collective-permute-start.19 = (bf16[2,4,16,896]{3,2,1,0:T(8,128)(2,1)}, bf16[2,4,16,896]{3,2,1,0:T(8,128)(2,1)S(1)}, u32[]{:S(2)}, u32[]{:S(2)}) collective-permute-start(bf16[2,4,16,896]{3,2,1,0:T(8,128)(2,1)} %slice.56), channel_id=1, source_target_pairs={{0,8},{8,16},{16,24},{24,0},{1,9},{9,17},{17,25},{25,1},{2,10},{10... | collective-permute-start | bytes 688136 | tf_op jit(solution)/shard_map/ppermute | solution.py:23
  37.4 2.4 %collective-permute-start.20 = (bf16[2,4,16,896]{3,2,1,0:T(8,128)(2,1)}, bf16[2,4,16,896]{3,2,1,0:T(8,128)(2,1)S(1)}, u32[]{:S(2)}, u32[]{:S(2)}) collective-permute-start(bf16[2,4,16,896]{3,2,1,0:T(8,128)(2,1)} %slice.57), channel_id=1, source_target_pairs={{0,24},{8,0},{16,8},{24,16},{1,25},{9,1},{17,9},{25,17},{2,26},{10... | collective-permute-start | bytes 688136 | tf_op jit(solution)/shard_map/ppermute | solution.py:23
  45.9 2.1 %collective-permute-done.19 = bf16[2,4,16,896]{3,2,1,0:T(8,128)(2,1)S(1)} collective-permute-done((bf16[2,4,16,896]{3,2,1,0:T(8,128)(2,1)}, bf16[2,4,16,896]{3,2,1,0:T(8,128)(2,1)S(1)}, u32[]{:S(2)}, u32[]{:S(2)}) %collective-permute-start.19) | collective-permute-done | bytes 229408 | tf_op jit(solution)/shard_map/ppermute | solution.py:23
  51.0 2.1 %collective-permute-start.14 = (bf16[512,256]{1,0:T(8,128)(2,1)}, bf16[512,256]{1,0:T(8,128)(2,1)}, u32[]{:S(2)}, u32[]{:S(2)}) collective-permute-start(bf16[512,256]{1,0:T(8,128)(2,1)} %param.18), channel_id=1, source_target_pairs={{0,96},{32,0},{64,32},{96,64},{1,97},{33,1},{65,33},{97,65},{2,98}... | collective-permute-start | bytes 786440 | tf_op jit(solution)/shard_map/ppermute | solution.py:23
  55.2 3.7 %pick.1.refs_0_ = bf16[32,16,896]{2,1,0:T(8,128)(2,1)S(1)} custom-call(s32[32]{0:T(128)S(1)} %fusion.11.place_ref, bf16[16,16,896]{2,1,0:T(8,128)(2,1)S(1)} %bitcast.32, bf16[16,16,896]{2,1,0:T(8,128)(2,1)S(1)} %bitcast.36, bf16[16,16,896]{2,1,0:T(8,128)(2,1)S(1)} %bitcast.35, bf16[8,16,896]{2,1,0:T(8,128)(2,1)S(1)} %bitcast.39, ...), custom_call_target="tpu_custom_call" | custom-call | bytes 2097152 | tf_op jit(solution)/shard_map/pick/pallas_call | solution.py:84
  58.9 3.1 %collective-permute-done.14 = bf16[512,256]{1,0:T(8,128)(2,1)} collective-permute-done((bf16[512,256]{1,0:T(8,128)(2,1)}, bf16[512,256]{1,0:T(8,128)(2,1)}, u32[]{:S(2)}, u32[]{:S(2)}) %collective-permute-start.14) | collective-permute-done | bytes 262176 | tf_op jit(solution)/shard_map/ppermute | solution.py:23
  64.9 2.5 %collective-permute-start.26 = (bf16[32,16,896]{2,1,0:T(8,128)(2,1)S(1)}, bf16[32,16,896]{2,1,0:T(8,128)(2,1)S(1)}, u32[]{:S(2)}, u32[]{:S(2)}) collective-permute-start(bf16[32,16,896]{2,1,0:T(8,128)(2,1)S(1)} %pick.1.refs_0_), channel_id=1, source_target_pairs={{0,6},{2,0},{4,2},{6,4},{1,7},{3,1},{5,3},{7,5},{8,14},{10,8},{12,... | collective-permute-start | bytes 2752520 | tf_op jit(solution)/shard_map/ppermute | solution.py:23
  71.1 2.1 %collective-permute-done.28.refs_2_ = bf16[4,56,1024]{2,1,0:T(8,128)(2,1)S(1)} collective-permute-done((bf16[4,56,1024]{2,1,0:T(8,128)(2,1)S(1)}, bf16[4,56,1024]{2,1,0:T(8,128)(2,1)S(1)}, u32[]{:S(2)}, u32[]{:S(2)}) %collective-permute-start.28) | collective-permute-done | bytes 458784 | tf_op jit(solution)/shard_map/ppermute | solution.py:23
  74.5 2.7 %collective-permute-done.27.refs_1_ = bf16[4,56,1024]{2,1,0:T(8,128)(2,1)S(1)} collective-permute-done((bf16[4,56,1024]{2,1,0:T(8,128)(2,1)S(1)}, bf16[4,56,1024]{2,1,0:T(8,128)(2,1)S(1)}, u32[]{:S(2)}, u32[]{:S(2)}) %collective-permute-start.27) | collective-permute-done | bytes 458784 | tf_op jit(solution)/shard_map/ppermute | solution.py:23
  77.3 6.4 %collective-permute-done.29.refs_3_ = bf16[2,56,1024]{2,1,0:T(8,128)(2,1)S(1)} collective-permute-done((bf16[2,56,1024]{2,1,0:T(8,128)(2,1)S(1)}, bf16[2,56,1024]{2,1,0:T(8,128)(2,1)S(1)}, u32[]{:S(2)}, u32[]{:S(2)}) %collective-permute-start.29) | collective-permute-done | bytes 229408 | tf_op jit(solution)/shard_map/ppermute | solution.py:23
  85.0 3.9 %collective-permute-done.30.refs_4_ = bf16[2,56,1024]{2,1,0:T(8,128)(2,1)S(1)} collective-permute-done((bf16[2,56,1024]{2,1,0:T(8,128)(2,1)S(1)}, bf16[2,56,1024]{2,1,0:T(8,128)(2,1)S(1)}, u32[]{:S(2)}, u32[]{:S(2)}) %collective-permute-start.30) | collective-permute-done | bytes 229408 | tf_op jit(solution)/shard_map/ppermute | solution.py:23
  90.4 3.0 %arrange.1 = bf16[16,56,1024]{2,1,0:T(8,128)(2,1)S(1)} custom-call(s32[16]{0:T(128)S(1)} %get-tuple-element.112.owner_ref, bf16[4,56,1024]{2,1,0:T(8,128)(2,1)S(1)} %pad_maximum_fusion.4.refs_0_, bf16[4,56,1024]{2,1,0:T(8,128)(2,1)S(1)} %collective-permute-done.27.refs_1_, bf16[4,56,1024]{2,1,0:T(8,128)(2,1)S(1)} %collective-permute-done.28.refs_2_, ...), custom_call_target="tpu_custom_call" | custom-call | bytes 4194304 | tf_op jit(solution)/shard_map/arrange/pallas_call | solution.py:108
  94.2 3.3 %collective-permute-start.31 = (bf16[2,256,512]{2,1,0:T(8,128)(2,1)S(1)}, bf16[2,256,512]{2,1,0:T(8,128)(2,1)S(1)}, u32[]{:S(2)}, u32[]{:S(2)}) collective-permute-start(bf16[2,256,512]{2,1,0:T(8,128)(2,1)S(1)} %slice.62), channel_id=1, source_target_pairs={{0,32},{32,64},{64,96},{96,0},{1,33},{33,65},{65,97},{97,1},{2,34}... | collective-permute-start | bytes 1572872 | tf_op jit(solution)/shard_map/ppermute | solution.py:23
  97.5 5.5 %collective-permute-done.33.refs_3_ = bf16[16,16,896]{2,1,0:T(8,128)(2,1)S(1)} collective-permute-done((bf16[16,16,896]{2,1,0:T(8,128)(2,1)S(1)}, bf16[16,16,896]{2,1,0:T(8,128)(2,1)S(1)}, u32[]{:S(2)}, u32[]{:S(2)}) %collective-permute-start.33) | collective-permute-done | bytes 458784 | tf_op jit(solution)/shard_map/ppermute | solution.py:23
  103.1 7.6 %collective-permute-done.34.refs_4_ = bf16[16,16,896]{2,1,0:T(8,128)(2,1)S(1)} collective-permute-done((bf16[16,16,896]{2,1,0:T(8,128)(2,1)S(1)}, bf16[16,16,896]{2,1,0:T(8,128)(2,1)S(1)}, u32[]{:S(2)}, u32[]{:S(2)}) %collective-permute-start.34) | collective-permute-done | bytes 458784 | tf_op jit(solution)/shard_map/ppermute | solution.py:23
  110.7 10.0 %collective-permute-start.37 = (bf16[32,16,896]{2,1,0:T(8,128)(2,1)S(1)}, bf16[32,16,896]{2,1,0:T(8,128)(2,1)S(1)}, u32[]{:S(2)}, u32[]{:S(2)}) collective-permute-start(bf16[32,16,896]{2,1,0:T(8,128)(2,1)S(1)} %pick.1.refs_0_), channel_id=1, source_target_pairs={{0,1},{1,0},{2,3},{3,2},{4,5},{5,4},{6,7},{7,6},{8,9},{9,8},{10,11... | collective-permute-start | bytes 2752520 | tf_op jit(solution)/shard_map/ppermute | solution.py:23
  121.3 6.7 %query_projection.1.query_ref = bf16[1024,512]{1,0:T(8,128)(2,1)S(1)} custom-call(s32[16]{0:T(128)S(1)} %get-tuple-element.111.owner_ref, bf16[1024,4096]{1,0:T(8,128)(2,1)S(1)} %bitcast.43, bf16[4,256,512]{2,1,0:T(8,128)(2,1)S(1)} %pad_maximum_fusion.refs_0_, bf16[4,256,512]{2,1,0:T(8,128)(2,1)S(1)} %collective-permute-done.23.refs_1_, ...), custom_call_target="tpu_custom_call" | custom-call | flops 4294967296 | bytes 14680064 | tf_op jit(solution)/shard_map/query_projection/pallas_call | solution.py:154
  132.7 6.9 %attend.2 = bf16[512,512]{1,0:T(8,128)(2,1)S(1)} custom-call(s32[4]{0:T(128)S(1)} %get-tuple-element.107.block_ref, bf16[1024,512]{1,0:T(8,128)(2,1)S(1)} %query_projection.1.query_ref, bf16[896,1024]{1,0:T(8,128)(2,1)S(1)} %bitcast.33, bf16[32,16,896]{2,1,0:T(8,128)(2,1)S(1)} %pick.1.refs_0_, bf16[32,16,896]{2,1,0:T(8,128)(2,1)S(1)} %collective-permute-done.25.refs_1_, ...), custom_call_target="tpu_custom_call" | custom-call | flops 6000000000 | bytes 12582912 | tf_op jit(solution)/shard_map/attend/pallas_call | solution.py:220
  139.6 6.9 %attend.3.mine_ref = bf16[512,512]{1,0:T(8,128)(2,1)S(1)} custom-call(s32[4]{0:T(128)S(1)} %broadcast_add_fusion.block_ref, bf16[1024,512]{1,0:T(8,128)(2,1)S(1)} %query_projection.1.query_ref, bf16[896,1024]{1,0:T(8,128)(2,1)S(1)} %bitcast.34, bf16[32,16,896]{2,1,0:T(8,128)(2,1)S(1)} %pick.1.refs_0_, ...), custom_call_target="tpu_custom_call" | custom-call | flops 6000000000 | bytes 12582912 | tf_op jit(solution)/shard_map/attend/pallas_call | solution.py:220
  149.2 4.9 %collective-permute-done.49.refs_9_ = bf16[2,512,256]{2,1,0:T(8,128)(2,1)S(1)} collective-permute-done((bf16[2,512,256]{2,1,0:T(8,128)(2,1)S(1)}, bf16[2,512,256]{2,1,0:T(8,128)(2,1)S(1)}, u32[]{:S(2)}, u32[]{:S(2)}) %collective-permute-start.49) | collective-permute-done | bytes 524320 | tf_op jit(solution)/shard_map/ppermute | solution.py:23
  154.9 4.5 %mix.1 = (bf16[128,2048]{1,0:T(8,128)(2,1)S(1)}, bf16[128,2048]{1,0:T(8,128)(2,1)S(1)}, bf16[128,2048]{1,0:T(8,128)(2,1)S(1)}, bf16[128,2048]{1,0:T(8,128)(2,1)S...) custom-call(bf16[512,512]{1,0:T(8,128)(2,1)S(1)} %attend.3.mine_ref,, ...), custom_call_target="tpu_custom_call" | custom-call | flops 4294967296 | bytes 14680064 | tf_op jit(solution)/shard_map/mix/pallas_call | solution.py:252
  159.5 2.7 %collective-permute-start.54 = (bf16[128,2048]{1,0:T(8,128)(2,1)S(1)}, bf16[128,2048]{1,0:T(8,128)(2,1)S(1)}, u32[]{:S(2)}, u32[]{:S(2)}) collective-permute-start(bf16[128,2048]{1,0:T(8,128)(2,1)S(1)} %get-tuple-element.106), channel_id=1, source_target_pairs={{0,6},{2,0},{4,2},{6,4},{1,7},{3,1},{5,3},{7,5},{8,14},{10,8},{12,... | collective-permute-start | bytes 1572872 | tf_op jit(solution)/shard_map/ppermute | solution.py:23
  163.6 10.2 %collective-permute-done.50 = bf16[128,2048]{1,0:T(8,128)(2,1)S(1)} collective-permute-done((bf16[128,2048]{1,0:T(8,128)(2,1)S(1)}, bf16[128,2048]{1,0:T(8,128)(2,1)S(1)}, u32[]{:S(2)}, u32[]{:S(2)}) %collective-permute-start.50) | collective-permute-done | bytes 524320 | tf_op jit(solution)/shard_map/ppermute | solution.py:23
  174.2 2.7 %collective-permute-start.55 = (bf16[128,2048]{1,0:T(8,128)(2,1)S(1)}, bf16[128,2048]{1,0:T(8,128)(2,1)S(1)}, u32[]{:S(2)}, u32[]{:S(2)}) collective-permute-start(bf16[128,2048]{1,0:T(8,128)(2,1)S(1)} %add_convert_fusion), channel_id=1, source_target_pairs={{0,6},{2,0},{4,2},{6,4},{1,7},{3,1},{5,3},{7,5},{8,14},{10,8},{12,... | collective-permute-start | bytes 1572872 | tf_op jit(solution)/shard_map/ppermute | solution.py:23
  176.9 7.1 %collective-permute-done.52.refs_2_ = bf16[128,2048]{1,0:T(8,128)(2,1)S(1)} collective-permute-done((bf16[128,2048]{1,0:T(8,128)(2,1)S(1)}, bf16[128,2048]{1,0:T(8,128)(2,1)S(1)}, u32[]{:S(2)}, u32[]{:S(2)}) %collective-permute-start.52) | collective-permute-done | bytes 524320 | tf_op jit(solution)/shard_map/ppermute | solution.py:23
  185.0 11.2 %collective-permute-done.51.refs_1_ = bf16[128,2048]{1,0:T(8,128)(2,1)S(1)} collective-permute-done((bf16[128,2048]{1,0:T(8,128)(2,1)S(1)}, bf16[128,2048]{1,0:T(8,128)(2,1)S(1)}, u32[]{:S(2)}, u32[]{:S(2)}) %collective-permute-start.51) | collective-permute-done | bytes 524320 | tf_op jit(solution)/shard_map/ppermute | solution.py:23
  (144 shorter events, 52.0 us)
Async XLA Ops:
  17.3 9.7 %collective-permute-start.6 = (bf16[4,4,16,896]{3,2,1,0:T(8,128)(2,1)S(1)}, bf16[4,4,16,896]{3,2,1,0:T(8,128)(2,1)S(1)}, u32[]{:S(2)}, u32[]{:S(2)}) collective-permute-start(bf16[4,4,16,896]{3,2,1,0:T(8,128)(2,1)S(1)} %pad_maximum_fusion.2), channel_id=1, source_target_pairs={{0,8},{8,16},{16,24},{24,0},{1,9},{9,17},{17,25},{25,1},{2,10},{10... | collective-permute-start | bytes 1376264 | tf_op jit(solution)/shard_map/ppermute | solution.py:23
  17.3 11.1 %collective-permute-start.9 = (bf16[4,4,16,896]{3,2,1,0:T(8,128)(2,1)S(1)}, bf16[4,4,16,896]{3,2,1,0:T(8,128)(2,1)S(1)}, u32[]{:S(2)}, u32[]{:S(2)}) collective-permute-start(bf16[4,4,16,896]{3,2,1,0:T(8,128)(2,1)S(1)} %pad_maximum_fusion.3), channel_id=1, source_target_pairs={{0,96},{32,0},{64,32},{96,64},{1,97},{33,1},{65,33},{97,65},{2,98}... | collective-permute-start | bytes 1376264 | tf_op jit(solution)/shard_map/ppermute | solution.py:23
  20.3 11.3 %collective-permute-start.8 = (bf16[4,4,16,896]{3,2,1,0:T(8,128)(2,1)S(1)}, bf16[4,4,16,896]{3,2,1,0:T(8,128)(2,1)S(1)}, u32[]{:S(2)}, u32[]{:S(2)}) collective-permute-start(bf16[4,4,16,896]{3,2,1,0:T(8,128)(2,1)S(1)} %pad_maximum_fusion.3), channel_id=1, source_target_pairs={{0,32},{32,64},{64,96},{96,0},{1,33},{33,65},{65,97},{97,1},{2,34}... | collective-permute-start | bytes 1376264 | tf_op jit(solution)/shard_map/ppermute | solution.py:23
  34.5 18.6 %collective-permute-start.12 = (bf16[256,512]{1,0:T(8,128)(2,1)}, bf16[256,512]{1,0:T(8,128)(2,1)}, u32[]{:S(2)}, u32[]{:S(2)}) collective-permute-start(bf16[256,512]{1,0:T(8,128)(2,1)} %param.15), channel_id=1, source_target_pairs={{0,16},{8,24},{16,0},{24,8},{1,17},{9,25},{17,1},{25,9},{2,18},{10... | collective-permute-start | bytes 786440 | tf_op jit(solution)/shard_map/ppermute | solution.py:23
  34.7 13.2 %collective-permute-start.19 = (bf16[2,4,16,896]{3,2,1,0:T(8,128)(2,1)}, bf16[2,4,16,896]{3,2,1,0:T(8,128)(2,1)S(1)}, u32[]{:S(2)}, u32[]{:S(2)}) collective-permute-start(bf16[2,4,16,896]{3,2,1,0:T(8,128)(2,1)} %slice.56), channel_id=1, source_target_pairs={{0,8},{8,16},{16,24},{24,0},{1,9},{9,17},{17,25},{25,1},{2,10},{10... | collective-permute-start | bytes 688136 | tf_op jit(solution)/shard_map/ppermute | solution.py:23
  37.4 10.6 %collective-permute-start.20 = (bf16[2,4,16,896]{3,2,1,0:T(8,128)(2,1)}, bf16[2,4,16,896]{3,2,1,0:T(8,128)(2,1)S(1)}, u32[]{:S(2)}, u32[]{:S(2)}) collective-permute-start(bf16[2,4,16,896]{3,2,1,0:T(8,128)(2,1)} %slice.57), channel_id=1, source_target_pairs={{0,24},{8,0},{16,8},{24,16},{1,25},{9,1},{17,9},{25,17},{2,26},{10... | collective-permute-start | bytes 688136 | tf_op jit(solution)/shard_map/ppermute | solution.py:23
  39.9 9.6 %collective-permute-start.21 = (bf16[2,4,16,896]{3,2,1,0:T(8,128)(2,1)}, bf16[2,4,16,896]{3,2,1,0:T(8,128)(2,1)S(1)}, u32[]{:S(2)}, u32[]{:S(2)}) collective-permute-start(bf16[2,4,16,896]{3,2,1,0:T(8,128)(2,1)} %slice.58), channel_id=1, source_target_pairs={{0,32},{32,64},{64,96},{96,0},{1,33},{33,65},{65,97},{97,1},{2,34}... | collective-permute-start | bytes 688136 | tf_op jit(solution)/shard_map/ppermute | solution.py:23
  41.2 9.9 %collective-permute-start.22 = (bf16[2,4,16,896]{3,2,1,0:T(8,128)(2,1)}, bf16[2,4,16,896]{3,2,1,0:T(8,128)(2,1)}, u32[]{:S(2)}, u32[]{:S(2)}) collective-permute-start(bf16[2,4,16,896]{3,2,1,0:T(8,128)(2,1)} %slice.59), channel_id=1, source_target_pairs={{0,96},{32,0},{64,32},{96,64},{1,97},{33,1},{65,33},{97,65},{2,98}... | collective-permute-start | bytes 688136 | tf_op jit(solution)/shard_map/ppermute | solution.py:23
  48.0 10.9 %collective-permute-start.11 = (bf16[256,512]{1,0:T(8,128)(2,1)}, bf16[256,512]{1,0:T(8,128)(2,1)}, u32[]{:S(2)}, u32[]{:S(2)}) collective-permute-start(bf16[256,512]{1,0:T(8,128)(2,1)} %param.15), channel_id=1, source_target_pairs={{0,24},{8,0},{16,8},{24,16},{1,25},{9,1},{17,9},{25,17},{2,26},{10... | collective-permute-start | bytes 786440 | tf_op jit(solution)/shard_map/ppermute | solution.py:23
  48.0 11.0 %collective-permute-start.10 = (bf16[256,512]{1,0:T(8,128)(2,1)}, bf16[256,512]{1,0:T(8,128)(2,1)}, u32[]{:S(2)}, u32[]{:S(2)}) collective-permute-start(bf16[256,512]{1,0:T(8,128)(2,1)} %param.15), channel_id=1, source_target_pairs={{0,8},{8,16},{16,24},{24,0},{1,9},{9,17},{17,25},{25,1},{2,10},{10... | collective-permute-start | bytes 786440 | tf_op jit(solution)/shard_map/ppermute | solution.py:23
  51.0 11.0 %collective-permute-start.14 = (bf16[512,256]{1,0:T(8,128)(2,1)}, bf16[512,256]{1,0:T(8,128)(2,1)}, u32[]{:S(2)}, u32[]{:S(2)}) collective-permute-start(bf16[512,256]{1,0:T(8,128)(2,1)} %param.18), channel_id=1, source_target_pairs={{0,96},{32,0},{64,32},{96,64},{1,97},{33,1},{65,33},{97,65},{2,98}... | collective-permute-start | bytes 786440 | tf_op jit(solution)/shard_map/ppermute | solution.py:23
  53.2 10.5 %collective-permute-start.13 = (bf16[512,256]{1,0:T(8,128)(2,1)}, bf16[512,256]{1,0:T(8,128)(2,1)}, u32[]{:S(2)}, u32[]{:S(2)}) collective-permute-start(bf16[512,256]{1,0:T(8,128)(2,1)} %param.18), channel_id=1, source_target_pairs={{0,32},{32,64},{64,96},{96,0},{1,33},{33,65},{65,97},{97,1},{2,34}... | collective-permute-start | bytes 786440 | tf_op jit(solution)/shard_map/ppermute | solution.py:23
  64.9 25.2 %collective-permute-start.26 = (bf16[32,16,896]{2,1,0:T(8,128)(2,1)S(1)}, bf16[32,16,896]{2,1,0:T(8,128)(2,1)S(1)}, u32[]{:S(2)}, u32[]{:S(2)}) collective-permute-start(bf16[32,16,896]{2,1,0:T(8,128)(2,1)S(1)} %pick.1.refs_0_), channel_id=1, source_target_pairs={{0,6},{2,0},{4,2},{6,4},{1,7},{3,1},{5,3},{7,5},{8,14},{10,8},{12,... | collective-permute-start | bytes 2752520 | tf_op jit(solution)/shard_map/ppermute | solution.py:23
  67.3 9.9 %collective-permute-start.27 = (bf16[4,56,1024]{2,1,0:T(8,128)(2,1)S(1)}, bf16[4,56,1024]{2,1,0:T(8,128)(2,1)S(1)}, u32[]{:S(2)}, u32[]{:S(2)}) collective-permute-start(bf16[4,56,1024]{2,1,0:T(8,128)(2,1)S(1)} %pad_maximum_fusion.4.refs_0_), channel_id=1, source_target_pairs={{0,8},{8,16},{16,24},{24,0},{1,9},{9,17},{17,25},{25,1},{2,10},{10... | collective-permute-start | bytes 1376264 | tf_op jit(solution)/shard_map/ppermute | solution.py:23
  69.1 24.4 %collective-permute-start.24 = (bf16[4,256,512]{2,1,0:T(8,128)(2,1)S(1)}, bf16[4,256,512]{2,1,0:T(8,128)(2,1)S(1)}, u32[]{:S(2)}, u32[]{:S(2)}) collective-permute-start(bf16[4,256,512]{2,1,0:T(8,128)(2,1)S(1)} %pad_maximum_fusion.refs_0_), channel_id=1, source_target_pairs={{0,96},{32,0},{64,32},{96,64},{1,97},{33,1},{65,33},{97,65},{2,98}... | collective-permute-start | bytes 3145736 | tf_op jit(solution)/shard_map/ppermute | solution.py:23
  71.1 23.0 %collective-permute-start.23 = (bf16[4,256,512]{2,1,0:T(8,128)(2,1)S(1)}, bf16[4,256,512]{2,1,0:T(8,128)(2,1)S(1)}, u32[]{:S(2)}, u32[]{:S(2)}) collective-permute-start(bf16[4,256,512]{2,1,0:T(8,128)(2,1)S(1)} %pad_maximum_fusion.refs_0_), channel_id=1, source_target_pairs={{0,32},{32,64},{64,96},{96,0},{1,33},{33,65},{65,97},{97,1},{2,34}... | collective-permute-start | bytes 3145736 | tf_op jit(solution)/shard_map/ppermute | solution.py:23
  73.3 20.1 %collective-permute-start.25 = (bf16[32,16,896]{2,1,0:T(8,128)(2,1)S(1)}, bf16[32,16,896]{2,1,0:T(8,128)(2,1)S(1)}, u32[]{:S(2)}, u32[]{:S(2)}) collective-permute-start(bf16[32,16,896]{2,1,0:T(8,128)(2,1)S(1)} %pick.1.refs_0_), channel_id=1, source_target_pairs={{0,2},{2,4},{4,6},{6,0},{1,3},{3,5},{5,7},{7,1},{8,10},{10,12},{12... | collective-permute-start | bytes 2752520 | tf_op jit(solution)/shard_map/ppermute | solution.py:23
  88.9 31.8 %collective-permute-start.36 = (bf16[4,512,256]{2,1,0:T(8,128)(2,1)S(1)}, bf16[4,512,256]{2,1,0:T(8,128)(2,1)S(1)}, u32[]{:S(2)}, u32[]{:S(2)}) collective-permute-start(bf16[4,512,256]{2,1,0:T(8,128)(2,1)S(1)} %pad_maximum_fusion.1.refs_0_), channel_id=1, source_target_pairs={{0,24},{8,0},{16,8},{24,16},{1,25},{9,1},{17,9},{25,17},{2,26},{10... | collective-permute-start | bytes 3145736 | tf_op jit(solution)/shard_map/ppermute | solution.py:23
  90.1 30.6 %collective-permute-start.35 = (bf16[4,512,256]{2,1,0:T(8,128)(2,1)S(1)}, bf16[4,512,256]{2,1,0:T(8,128)(2,1)S(1)}, u32[]{:S(2)}, u32[]{:S(2)}) collective-permute-start(bf16[4,512,256]{2,1,0:T(8,128)(2,1)S(1)} %pad_maximum_fusion.1.refs_0_), channel_id=1, source_target_pairs={{0,8},{8,16},{16,24},{24,0},{1,9},{9,17},{17,25},{25,1},{2,10},{10... | collective-permute-start | bytes 3145736 | tf_op jit(solution)/shard_map/ppermute | solution.py:23
  94.2 27.1 %collective-permute-start.31 = (bf16[2,256,512]{2,1,0:T(8,128)(2,1)S(1)}, bf16[2,256,512]{2,1,0:T(8,128)(2,1)S(1)}, u32[]{:S(2)}, u32[]{:S(2)}) collective-permute-start(bf16[2,256,512]{2,1,0:T(8,128)(2,1)S(1)} %slice.62), channel_id=1, source_target_pairs={{0,32},{32,64},{64,96},{96,0},{1,33},{33,65},{65,97},{97,1},{2,34}... | collective-permute-start | bytes 1572872 | tf_op jit(solution)/shard_map/ppermute | solution.py:23
  97.5 23.8 %collective-permute-start.32 = (bf16[2,256,512]{2,1,0:T(8,128)(2,1)S(1)}, bf16[2,256,512]{2,1,0:T(8,128)(2,1)S(1)}, u32[]{:S(2)}, u32[]{:S(2)}) collective-permute-start(bf16[2,256,512]{2,1,0:T(8,128)(2,1)S(1)} %slice.63), channel_id=1, source_target_pairs={{0,96},{32,0},{64,32},{96,64},{1,97},{33,1},{65,33},{97,65},{2,98}... | collective-permute-start | bytes 1572872 | tf_op jit(solution)/shard_map/ppermute | solution.py:23
  110.7 22.0 %collective-permute-start.37 = (bf16[32,16,896]{2,1,0:T(8,128)(2,1)S(1)}, bf16[32,16,896]{2,1,0:T(8,128)(2,1)S(1)}, u32[]{:S(2)}, u32[]{:S(2)}) collective-permute-start(bf16[32,16,896]{2,1,0:T(8,128)(2,1)S(1)} %pick.1.refs_0_), channel_id=1, source_target_pairs={{0,1},{1,0},{2,3},{3,2},{4,5},{5,4},{6,7},{7,6},{8,9},{9,8},{10,11... | collective-permute-start | bytes 2752520 | tf_op jit(solution)/shard_map/ppermute | solution.py:23
  120.7 12.0 %collective-permute-start.38 = (bf16[32,16,896]{2,1,0:T(8,128)(2,1)S(1)}, bf16[32,16,896]{2,1,0:T(8,128)(2,1)S(1)}, u32[]{:S(2)}, u32[]{:S(2)}) collective-permute-start(bf16[32,16,896]{2,1,0:T(8,128)(2,1)S(1)} %collective-permute-done.25.refs_1_), channel_id=1, source_target_pairs={{0,1},{1,0},{2,3},{3,2},{4,5},{5,4},{6,7},{7,6},{8,9},{9,8},{10,11... | collective-permute-start | bytes 2752520 | tf_op jit(solution)/shard_map/ppermute | solution.py:23
  120.7 12.0 %collective-permute-start.39 = (bf16[32,16,896]{2,1,0:T(8,128)(2,1)S(1)}, bf16[32,16,896]{2,1,0:T(8,128)(2,1)S(1)}, u32[]{:S(2)}, u32[]{:S(2)}) collective-permute-start(bf16[32,16,896]{2,1,0:T(8,128)(2,1)S(1)} %collective-permute-done.26.refs_2_), channel_id=1, source_target_pairs={{0,1},{1,0},{2,3},{3,2},{4,5},{5,4},{6,7},{7,6},{8,9},{9,8},{10,11... | collective-permute-start | bytes 2752520 | tf_op jit(solution)/shard_map/ppermute | solution.py:23
  130.0 16.6 %collective-permute-start.43 = (bf16[2,512,256]{2,1,0:T(8,128)(2,1)S(1)}, bf16[2,512,256]{2,1,0:T(8,128)(2,1)S(1)}, u32[]{:S(2)}, u32[]{:S(2)}) collective-permute-start(bf16[2,512,256]{2,1,0:T(8,128)(2,1)S(1)} %slice.66), channel_id=1, source_target_pairs={{0,8},{8,16},{16,24},{24,0},{1,9},{9,17},{17,25},{25,1},{2,10},{10... | collective-permute-start | bytes 1572872 | tf_op jit(solution)/shard_map/ppermute | solution.py:23
  130.6 15.9 %collective-permute-start.44 = (bf16[2,512,256]{2,1,0:T(8,128)(2,1)S(1)}, bf16[2,512,256]{2,1,0:T(8,128)(2,1)S(1)}, u32[]{:S(2)}, u32[]{:S(2)}) collective-permute-start(bf16[2,512,256]{2,1,0:T(8,128)(2,1)S(1)} %slice.67), channel_id=1, source_target_pairs={{0,24},{8,0},{16,8},{24,16},{1,25},{9,1},{17,9},{25,17},{2,26},{10... | collective-permute-start | bytes 1572872 | tf_op jit(solution)/shard_map/ppermute | solution.py:23
  159.4 14.4 %collective-permute-start.50 = (bf16[128,2048]{1,0:T(8,128)(2,1)S(1)}, bf16[128,2048]{1,0:T(8,128)(2,1)S(1)}, u32[]{:S(2)}, u32[]{:S(2)}) collective-permute-start(bf16[128,2048]{1,0:T(8,128)(2,1)S(1)} %get-tuple-element.101), channel_id=1, source_target_pairs={{0,2},{2,4},{4,6},{6,0},{1,3},{3,5},{5,7},{7,1},{8,10},{10,12},{12... | collective-permute-start | bytes 1572872 | tf_op jit(solution)/shard_map/ppermute | solution.py:23
  159.5 14.6 %collective-permute-start.54 = (bf16[128,2048]{1,0:T(8,128)(2,1)S(1)}, bf16[128,2048]{1,0:T(8,128)(2,1)S(1)}, u32[]{:S(2)}, u32[]{:S(2)}) collective-permute-start(bf16[128,2048]{1,0:T(8,128)(2,1)S(1)} %get-tuple-element.106), channel_id=1, source_target_pairs={{0,6},{2,0},{4,2},{6,4},{1,7},{3,1},{5,3},{7,5},{8,14},{10,8},{12,... | collective-permute-start | bytes 1572872 | tf_op jit(solution)/shard_map/ppermute | solution.py:23
  162.1 21.8 %collective-permute-start.52 = (bf16[128,2048]{1,0:T(8,128)(2,1)S(1)}, bf16[128,2048]{1,0:T(8,128)(2,1)S(1)}, u32[]{:S(2)}, u32[]{:S(2)}) collective-permute-start(bf16[128,2048]{1,0:T(8,128)(2,1)S(1)} %get-tuple-element.102), channel_id=1, source_target_pairs={{0,6},{2,0},{4,2},{6,4},{1,7},{3,1},{5,3},{7,5},{8,14},{10,8},{12,... | collective-permute-start | bytes 1572872 | tf_op jit(solution)/shard_map/ppermute | solution.py:23
  162.2 22.9 %collective-permute-start.53 = (bf16[128,2048]{1,0:T(8,128)(2,1)S(1)}, bf16[128,2048]{1,0:T(8,128)(2,1)S(1)}, u32[]{:S(2)}, u32[]{:S(2)}) collective-permute-start(bf16[128,2048]{1,0:T(8,128)(2,1)S(1)} %get-tuple-element.104), channel_id=1, source_target_pairs={{0,2},{2,4},{4,6},{6,0},{1,3},{3,5},{5,7},{7,1},{8,10},{10,12},{12... | collective-permute-start | bytes 1572872 | tf_op jit(solution)/shard_map/ppermute | solution.py:23
  173.9 22.3 %collective-permute-start.51 = (bf16[128,2048]{1,0:T(8,128)(2,1)S(1)}, bf16[128,2048]{1,0:T(8,128)(2,1)S(1)}, u32[]{:S(2)}, u32[]{:S(2)}) collective-permute-start(bf16[128,2048]{1,0:T(8,128)(2,1)S(1)} %add_convert_fusion.1), channel_id=1, source_target_pairs={{0,2},{2,4},{4,6},{6,0},{1,3},{3,5},{5,7},{7,1},{8,10},{10,12},{12... | collective-permute-start | bytes 1572872 | tf_op jit(solution)/shard_map/ppermute | solution.py:23
  174.2 22.1 %collective-permute-start.55 = (bf16[128,2048]{1,0:T(8,128)(2,1)S(1)}, bf16[128,2048]{1,0:T(8,128)(2,1)S(1)}, u32[]{:S(2)}, u32[]{:S(2)}) collective-permute-start(bf16[128,2048]{1,0:T(8,128)(2,1)S(1)} %add_convert_fusion), channel_id=1, source_target_pairs={{0,6},{2,0},{4,2},{6,4},{1,7},{3,1},{5,3},{7,5},{8,14},{10,8},{12,... | collective-permute-start | bytes 1572872 | tf_op jit(solution)/shard_map/ppermute | solution.py:23
  (38 other events, 380.8 us)

commit v3 on v2

--- a/solution.py
+++ b/solution.py
@@ -236,27 +236,30 @@
 
 
 def mix_kernel(mine_ref, other_ref, *refs):
-    mine_w, other_w, outs = refs[:5], refs[5:10], refs[10:]
+    outs = refs[-4:]
+    count = (len(refs) - 4) // 2
     rows = mine_ref.shape[0] // 4
-    for j, (p, s) in enumerate(BLOCKS):
-        total = jnp.dot(mine_ref[...], mine_w[p][s], preferred_element_type=jnp.float32)
-        total += jnp.dot(other_ref[...], other_w[p][s], preferred_element_type=jnp.float32)
-        total = total.astype(jnp.bfloat16)
-        at = j % 8 * 256
-        for k in range(4):
-            outs[k * 2 + j // 8][:, at : at + 256] = total[k * rows : (k + 1) * rows]
+    at = 0
+    for mine_w, other_w in zip(refs[:count], refs[count:-4]):
+        for s in range(mine_w.shape[0]):
+            total = jnp.dot(mine_ref[...], mine_w[s], preferred_element_type=jnp.float32)
+            total += jnp.dot(other_ref[...], other_w[s], preferred_element_type=jnp.float32)
+            total = total.astype(jnp.bfloat16)
+            for k in range(4):
+                outs[k][:, at : at + 256] = total[k * rows : (k + 1) * rows]
+            at += 256
 
 
 def mix(mine, other, mine_w, other_w):
     shape = jax.ShapeDtypeStruct((128, 2048), jnp.bfloat16)
     return pl.pallas_call(
         mix_kernel,
-        out_shape=[shape] * 8,
-        in_specs=[VMEM] * 12,
-        out_specs=[VMEM] * 8,
-        compiler_params=pltpu.CompilerParams(vmem_limit_bytes=24 * MIB),
+        out_shape=[shape] * 4,
+        in_specs=[VMEM] * (2 + 2 * len(mine_w)),
+        out_specs=[VMEM] * 4,
+        compiler_params=pltpu.CompilerParams(vmem_limit_bytes=16 * MIB),
         cost_estimate=pl.CostEstimate(
-            flops=2 * 512 * 1024 * 4096, bytes_accessed=14 * MIB, transcendentals=0
+            flops=2 * 512 * 1024 * 2048, bytes_accessed=7 * MIB, transcendentals=0
         ),
         name="mix",
     )(mine, other, *mine_w, *other_w)
@@ -334,21 +337,21 @@
     halves = hold(far_halves(near_x) + far_halves(q_near), panel)
     pieces = hold(ring_far(near_x, halves[:2], "x"), *halves)
     q_far = ring_far(q_near, halves[2:], "z")
-    query = query_projection(by_yz, tokens, q_far)
-    halves = hold(far_halves(o_near), query)
+    query = query_projection(by_yz, tokens, hold(q_far, *pieces[3:]))
+    halves = hold(far_halves(o_near), *pieces[3:])
     o_all = ring_far(o_near, halves, "y")
     pieces = pieces[:3] + hold(pieces[3:], *halves)
     pieces += [shift(p, "core", 1) for p in pieces]
     chips = (x + jnp.array([2, 1, 3, 0], jnp.int32)) % RING
     give = attend((chips * 2 + 1 - core).astype(jnp.int32), query, panel, pieces)
     other = shift(give, "core", 1)
-    o_other = [shift(w, "core", 1) for w in hold(o_all[:3], give)]
-    mine = attend((chips * 2 + core).astype(jnp.int32), after(query, give), panel, pieces)
-    o_other += [shift(w, "core", 1) for w in hold(o_all[3:], mine)]
-    t2a, t2b, t1a, t1b, t3a, t3b, t0a, t0b = mix(mine, other, o_all, o_other)
-
-    to_next, to_last = shift(t2a, "x", 1), shift(t2b, "x", -1)
-    r1b, r3a = shift(t1b, "x", 1), shift(t3a, "x", -1)
+    o_other = [shift(w, "core", 1) for w in hold(o_all, give)]
+    late = after(query, give, *o_all[3:])
+    mine = attend((chips * 2 + core).astype(jnp.int32), late, panel, pieces)
+    t2a, t1a, t3a, t0a = mix(mine, other, o_all[:2], o_other[:2])
+    to_next, r3a = shift(t2a, "x", 1), shift(t3a, "x", -1)
+    t2b, t1b, t3b, t0b = mix(after(mine, t2a), other, o_all[2:], o_other[2:])
+    to_last, r1b = shift(t2b, "x", -1), shift(t1b, "x", 1)
     r1a = shift(added(t1a, to_next), "x", 1)
     r3b = shift(added(t3b, to_last), "x", -1)
     return final(by_zy, [t0a, r1a, r3a, t0b, r1b, r3b])

time: 198 us -> 197 us (level)
  waiting for transfers between devices: 87 us -> 66.6 us
  starting transfers between devices: 64 us -> 83.1 us
    ppermute x56, waiting for transfers between devices: 87 us -> 66.6 us  [shift(): lax.ppermute(value, axis, [(i, (i + step) % size) for i in range(size)])]
    ppermute x56, starting transfers between devices: 64 us -> 83.1 us  [shift(): lax.ppermute(value, axis, [(i, (i + step) % size) for i in range(size)])]
    pallas_call x1 -> x2, Pallas kernels: 4.51 us -> 4.67 us  [mix(): pl.pallas_call(mix_kernel, out_shape=[shape] * 4, in_specs=[VMEM] * (2 +...]
  transfers between devices with their start and end apart: 56 -> 56, of which waited for: 27 -> 19; matrix products, arithmetic and copies ran while one was open for 5% -> 5% of each run, Pallas kernels for 14% -> 16%
where the time goes in v3:
time: 197 us; the launch traced here: 196 us
  starting transfers between devices  83.1 us (42%)
  waiting for transfers between devices  66.6 us (34%)
  Pallas kernels  33.7 us (17%)
  local copies, waits for them, and re-layouts  7.45 us (4%)
  other arithmetic  5.09 us (3%)
    ppermute x56, starting transfers between devices, shift(): lax.ppermute(value, axis, [(i, (i + step) % size) for i in range(size)])  83.1 us
    ppermute x56, waiting for transfers between devices, shift(): lax.ppermute(value, axis, [(i, (i + step) % size) for i in range(size)])  66.6 us
    pallas_call x2, Pallas kernels, attend(): pl.pallas_call(attend_kernel, out_shape=jax.ShapeDtypeStruct((count * blo...  13.8 us
    pallas_call x1, Pallas kernels, query_projection(): pl.pallas_call(query_kernel, out_shape=jax.ShapeDtypeStruct((rows, width)...  6.71 us
    pallas_call x2, Pallas kernels, mix(): pl.pallas_call(mix_kernel, out_shape=[shape] * 4, in_specs=[VMEM] * (2 +...  4.67 us
  transfers between devices with their start and end apart: 56, of which 19 were waited for; matrix products, arithmetic and copies ran while one was open for 5% of the time, Pallas kernels for 16%

profile of v3, /device:TPU:1, one launch (start us, length us, event | category | flops | bytes accessed | tf_op | source)
XLA Modules:
  0.0 196.4 jit_solution(18432520052113002251)
XLA Ops:
  1.0 4.5 %collective-permute-start.2 = (bf16[4,16,896]{2,1,0:T(8,128)(2,1)S(1)}, bf16[4,16,896]{2,1,0:T(8,128)(2,1)S(1)}, u32[]{:S(2)}, u32[]{:S(2)}) collective-permute-start(bf16[4,16,896]{2,1,0:T(8,128)(2,1)S(1)} %get-tuple-element.122), channel_id=1, source_target_pairs={{0,64},{32,96},{64,0},{96,32},{1,65},{33,97},{65,1},{97,33},{2,66}... | collective-permute-start | bytes 344072 | tf_op jit(solution)/shard_map/ppermute | solution.py:23
  7.0 2.9 %collective-permute-start.5 = (bf16[4,16,896]{2,1,0:T(8,128)(2,1)S(1)}, bf16[4,16,896]{2,1,0:T(8,128)(2,1)S(1)}, u32[]{:S(2)}, u32[]{:S(2)}) collective-permute-start(bf16[4,16,896]{2,1,0:T(8,128)(2,1)S(1)} %get-tuple-element.121), channel_id=1, source_target_pairs={{0,16},{8,24},{16,0},{24,8},{1,17},{9,25},{17,1},{25,9},{2,18},{10... | collective-permute-start | bytes 344072 | tf_op jit(solution)/shard_map/ppermute | solution.py:23
  12.1 2.3 %collective-permute-done.4 = bf16[4,16,896]{2,1,0:T(8,128)(2,1)S(1)} collective-permute-done((bf16[4,16,896]{2,1,0:T(8,128)(2,1)S(1)}, bf16[4,16,896]{2,1,0:T(8,128)(2,1)S(1)}, u32[]{:S(2)}, u32[]{:S(2)}) %collective-permute-start.4) | collective-permute-done | bytes 114720 | tf_op jit(solution)/shard_map/ppermute | solution.py:23
  16.2 2.5 %collective-permute-start.7 = (bf16[4,4,16,896]{3,2,1,0:T(8,128)(2,1)S(1)}, bf16[4,4,16,896]{3,2,1,0:T(8,128)(2,1)S(1)}, u32[]{:S(2)}, u32[]{:S(2)}) collective-permute-start(bf16[4,4,16,896]{3,2,1,0:T(8,128)(2,1)S(1)} %pad_maximum_fusion.2), channel_id=1, source_target_pairs={{0,24},{8,0},{16,8},{24,16},{1,25},{9,1},{17,9},{25,17},{2,26},{10... | collective-permute-start | bytes 1376264 | tf_op jit(solution)/shard_map/ppermute | solution.py:23
  21.4 5.0 %collective-permute-done.6 = bf16[4,4,16,896]{3,2,1,0:T(8,128)(2,1)S(1)} collective-permute-done((bf16[4,4,16,896]{3,2,1,0:T(8,128)(2,1)S(1)}, bf16[4,4,16,896]{3,2,1,0:T(8,128)(2,1)S(1)}, u32[]{:S(2)}, u32[]{:S(2)}) %collective-permute-start.6) | collective-permute-done | bytes 458784 | tf_op jit(solution)/shard_map/ppermute | solution.py:23
  30.0 2.7 %collective-permute-start.17 = (bf16[56,1024]{1,0:T(8,128)(2,1)S(1)}, bf16[56,1024]{1,0:T(8,128)(2,1)S(1)}, u32[]{:S(2)}, u32[]{:S(2)}) collective-permute-start(bf16[56,1024]{1,0:T(8,128)(2,1)S(1)} %pad_maximum_fusion.5), channel_id=1, source_target_pairs={{0,96},{32,0},{64,32},{96,64},{1,97},{33,1},{65,33},{97,65},{2,98}... | collective-permute-start | bytes 344072 | tf_op jit(solution)/shard_map/ppermute | solution.py:23
  44.3 2.5 %collective-permute-start.14 = (bf16[512,256]{1,0:T(8,128)(2,1)}, bf16[512,256]{1,0:T(8,128)(2,1)}, u32[]{:S(2)}, u32[]{:S(2)}) collective-permute-start(bf16[512,256]{1,0:T(8,128)(2,1)} %param.18), channel_id=1, source_target_pairs={{0,96},{32,0},{64,32},{96,64},{1,97},{33,1},{65,33},{97,65},{2,98}... | collective-permute-start | bytes 786440 | tf_op jit(solution)/shard_map/ppermute | solution.py:23
  49.1 3.6 %pick.1.refs_0_ = bf16[32,16,896]{2,1,0:T(8,128)(2,1)S(1)} custom-call(s32[32]{0:T(128)S(1)} %fusion.11.place_ref, bf16[16,16,896]{2,1,0:T(8,128)(2,1)S(1)} %bitcast.31, bf16[16,16,896]{2,1,0:T(8,128)(2,1)S(1)} %bitcast.35, bf16[16,16,896]{2,1,0:T(8,128)(2,1)S(1)} %bitcast.36, bf16[8,16,896]{2,1,0:T(8,128)(2,1)S(1)} %bitcast.39, ...), custom_call_target="tpu_custom_call" | custom-call | bytes 2097152 | tf_op jit(solution)/shard_map/pick/pallas_call | solution.py:84
  52.8 2.2 %collective-permute-done.14 = bf16[512,256]{1,0:T(8,128)(2,1)} collective-permute-done((bf16[512,256]{1,0:T(8,128)(2,1)}, bf16[512,256]{1,0:T(8,128)(2,1)}, u32[]{:S(2)}, u32[]{:S(2)}) %collective-permute-start.14) | collective-permute-done | bytes 262176 | tf_op jit(solution)/shard_map/ppermute | solution.py:23
  55.2 2.7 %collective-permute-start.28 = (bf16[4,56,1024]{2,1,0:T(8,128)(2,1)S(1)}, bf16[4,56,1024]{2,1,0:T(8,128)(2,1)S(1)}, u32[]{:S(2)}, u32[]{:S(2)}) collective-permute-start(bf16[4,56,1024]{2,1,0:T(8,128)(2,1)S(1)} %pad_maximum_fusion.4.refs_0_), channel_id=1, source_target_pairs={{0,24},{8,0},{16,8},{24,16},{1,25},{9,1},{17,9},{25,17},{2,26},{10... | collective-permute-start | bytes 1376264 | tf_op jit(solution)/shard_map/ppermute | solution.py:23
  64.2 2.5 %collective-permute-start.26 = (bf16[32,16,896]{2,1,0:T(8,128)(2,1)S(1)}, bf16[32,16,896]{2,1,0:T(8,128)(2,1)S(1)}, u32[]{:S(2)}, u32[]{:S(2)}) collective-permute-start(bf16[32,16,896]{2,1,0:T(8,128)(2,1)S(1)} %pick.1.refs_0_), channel_id=1, source_target_pairs={{0,6},{2,0},{4,2},{6,4},{1,7},{3,1},{5,3},{7,5},{8,14},{10,8},{12,... | collective-permute-start | bytes 2752520 | tf_op jit(solution)/shard_map/ppermute | solution.py:23
  66.8 8.9 %collective-permute-done.29.refs_3_ = bf16[2,56,1024]{2,1,0:T(8,128)(2,1)S(1)} collective-permute-done((bf16[2,56,1024]{2,1,0:T(8,128)(2,1)S(1)}, bf16[2,56,1024]{2,1,0:T(8,128)(2,1)S(1)}, u32[]{:S(2)}, u32[]{:S(2)}) %collective-permute-start.29) | collective-permute-done | bytes 229408 | tf_op jit(solution)/shard_map/ppermute | solution.py:23
  76.9 3.9 %collective-permute-done.30.refs_4_ = bf16[2,56,1024]{2,1,0:T(8,128)(2,1)S(1)} collective-permute-done((bf16[2,56,1024]{2,1,0:T(8,128)(2,1)S(1)}, bf16[2,56,1024]{2,1,0:T(8,128)(2,1)S(1)}, u32[]{:S(2)}, u32[]{:S(2)}) %collective-permute-start.30) | collective-permute-done | bytes 229408 | tf_op jit(solution)/shard_map/ppermute | solution.py:23
  80.8 2.7 %collective-permute-start.36 = (bf16[4,512,256]{2,1,0:T(8,128)(2,1)S(1)}, bf16[4,512,256]{2,1,0:T(8,128)(2,1)S(1)}, u32[]{:S(2)}, u32[]{:S(2)}) collective-permute-start(bf16[4,512,256]{2,1,0:T(8,128)(2,1)S(1)} %pad_maximum_fusion.1.refs_0_), channel_id=1, source_target_pairs={{0,24},{8,0},{16,8},{24,16},{1,25},{9,1},{17,9},{25,17},{2,26},{10... | collective-permute-start | bytes 3145736 | tf_op jit(solution)/shard_map/ppermute | solution.py:23
  83.6 3.0 %arrange.1 = bf16[16,56,1024]{2,1,0:T(8,128)(2,1)S(1)} custom-call(s32[16]{0:T(128)S(1)} %get-tuple-element.124.owner_ref, bf16[4,56,1024]{2,1,0:T(8,128)(2,1)S(1)} %pad_maximum_fusion.4.refs_0_, bf16[4,56,1024]{2,1,0:T(8,128)(2,1)S(1)} %collective-permute-done.27.refs_1_, bf16[4,56,1024]{2,1,0:T(8,128)(2,1)S(1)} %collective-permute-done.28.refs_2_, ...), custom_call_target="tpu_custom_call" | custom-call | bytes 4194304 | tf_op jit(solution)/shard_map/arrange/pallas_call | solution.py:108
  86.8 2.7 %collective-permute-start.34 = (bf16[16,16,896]{2,1,0:T(8,128)(2,1)S(1)}, bf16[16,16,896]{2,1,0:T(8,128)(2,1)S(1)}, u32[]{:S(2)}, u32[]{:S(2)}) collective-permute-start(bf16[16,16,896]{2,1,0:T(8,128)(2,1)S(1)} %slice.61), channel_id=1, source_target_pairs={{0,6},{2,0},{4,2},{6,4},{1,7},{3,1},{5,3},{7,5},{8,14},{10,8},{12,... | collective-permute-start | bytes 1376264 | tf_op jit(solution)/shard_map/ppermute | solution.py:23
  90.4 5.0 %collective-permute-done.33.refs_3_ = bf16[16,16,896]{2,1,0:T(8,128)(2,1)S(1)} collective-permute-done((bf16[16,16,896]{2,1,0:T(8,128)(2,1)S(1)}, bf16[16,16,896]{2,1,0:T(8,128)(2,1)S(1)}, u32[]{:S(2)}, u32[]{:S(2)}) %collective-permute-start.33) | collective-permute-done | bytes 458784 | tf_op jit(solution)/shard_map/ppermute | solution.py:23
  95.4 3.0 %collective-permute-start.32 = (bf16[2,256,512]{2,1,0:T(8,128)(2,1)S(1)}, bf16[2,256,512]{2,1,0:T(8,128)(2,1)S(1)}, u32[]{:S(2)}, u32[]{:S(2)}) collective-permute-start(bf16[2,256,512]{2,1,0:T(8,128)(2,1)S(1)} %slice.63), channel_id=1, source_target_pairs={{0,96},{32,0},{64,32},{96,64},{1,97},{33,1},{65,33},{97,65},{2,98}... | collective-permute-start | bytes 1572872 | tf_op jit(solution)/shard_map/ppermute | solution.py:23
  98.4 17.8 %collective-permute-start.37 = (bf16[32,16,896]{2,1,0:T(8,128)(2,1)S(1)}, bf16[32,16,896]{2,1,0:T(8,128)(2,1)S(1)}, u32[]{:S(2)}, u32[]{:S(2)}) collective-permute-start(bf16[32,16,896]{2,1,0:T(8,128)(2,1)S(1)} %pick.1.refs_0_), channel_id=1, source_target_pairs={{0,1},{1,0},{2,3},{3,2},{4,5},{5,4},{6,7},{7,6},{8,9},{9,8},{10,11... | collective-permute-start | bytes 2752520 | tf_op jit(solution)/shard_map/ppermute | solution.py:23
  117.0 5.9 %collective-permute-start.41 = (bf16[16,16,896]{2,1,0:T(8,128)(2,1)S(1)}, bf16[16,16,896]{2,1,0:T(8,128)(2,1)S(1)}, u32[]{:S(2)}, u32[]{:S(2)}) collective-permute-start(bf16[16,16,896]{2,1,0:T(8,128)(2,1)S(1)} %collective-permute-done.34.refs_4_), channel_id=1, source_target_pairs={{0,1},{1,0},{2,3},{3,2},{4,5},{5,4},{6,7},{7,6},{8,9},{9,8},{10,11... | collective-permute-start | bytes 1376264 | tf_op jit(solution)/shard_map/ppermute | solution.py:23
  122.9 6.7 %query_projection.1.query_ref = bf16[1024,512]{1,0:T(8,128)(2,1)S(1)} custom-call(s32[16]{0:T(128)S(1)} %get-tuple-element.123.owner_ref, bf16[1024,4096]{1,0:T(8,128)(2,1)S(1)} %bitcast.43, bf16[4,256,512]{2,1,0:T(8,128)(2,1)S(1)} %pad_maximum_fusion.refs_0_, bf16[4,256,512]{2,1,0:T(8,128)(2,1)S(1)} %collective-permute-done.23.refs_1_, ...), custom_call_target="tpu_custom_call" | custom-call | flops 4294967296 | bytes 14680064 | tf_op jit(solution)/shard_map/query_projection/pallas_call | solution.py:154
  129.8 2.7 %collective-permute-start.43 = (bf16[2,512,256]{2,1,0:T(8,128)(2,1)S(1)}, bf16[2,512,256]{2,1,0:T(8,128)(2,1)S(1)}, u32[]{:S(2)}, u32[]{:S(2)}) collective-permute-start(bf16[2,512,256]{2,1,0:T(8,128)(2,1)S(1)} %slice.67), channel_id=1, source_target_pairs={{0,24},{8,0},{16,8},{24,16},{1,25},{9,1},{17,9},{25,17},{2,26},{10... | collective-permute-start | bytes 1572872 | tf_op jit(solution)/shard_map/ppermute | solution.py:23
  132.4 6.9 %attend.2 = bf16[512,512]{1,0:T(8,128)(2,1)S(1)} custom-call(s32[4]{0:T(128)S(1)} %get-tuple-element.119.block_ref, bf16[1024,512]{1,0:T(8,128)(2,1)S(1)} %query_projection.1.query_ref, bf16[896,1024]{1,0:T(8,128)(2,1)S(1)} %bitcast.33, bf16[32,16,896]{2,1,0:T(8,128)(2,1)S(1)} %pick.1.refs_0_, bf16[32,16,896]{2,1,0:T(8,128)(2,1)S(1)} %collective-permute-done.25.refs_1_, ...), custom_call_target="tpu_custom_call" | custom-call | flops 6000000000 | bytes 12582912 | tf_op jit(solution)/shard_map/attend/pallas_call | solution.py:220
  140.0 4.5 %collective-permute-done.42.refs_1_ = bf16[2,512,256]{2,1,0:T(8,128)(2,1)S(1)} collective-permute-done((bf16[2,512,256]{2,1,0:T(8,128)(2,1)S(1)}, bf16[2,512,256]{2,1,0:T(8,128)(2,1)S(1)}, u32[]{:S(2)}, u32[]{:S(2)}) %collective-permute-start.42) | collective-permute-done | bytes 524320 | tf_op jit(solution)/shard_map/ppermute | solution.py:23
  146.3 6.9 %attend.3.mine_ref = bf16[512,512]{1,0:T(8,128)(2,1)S(1)} custom-call(s32[4]{0:T(128)S(1)} %broadcast_add_fusion.block_ref, bf16[1024,512]{1,0:T(8,128)(2,1)S(1)} %query_projection.1.query_ref, bf16[896,1024]{1,0:T(8,128)(2,1)S(1)} %bitcast.34, bf16[32,16,896]{2,1,0:T(8,128)(2,1)S(1)} %pick.1.refs_0_, ...), custom_call_target="tpu_custom_call" | custom-call | flops 6000000000 | bytes 12582912 | tf_op jit(solution)/shard_map/attend/pallas_call | solution.py:220
  153.3 2.3 %mix.2 = (bf16[128,2048]{1,0:T(8,128)(2,1)S(1)}, bf16[128,2048]{1,0:T(8,128)(2,1)S(1)}, bf16[128,2048]{1,0:T(8,128)(2,1)S(1)}, bf16[128,2048]{1,0:T(8,128)(2,1)S(1)}) custom-call(bf16[512,512]{1,0:T(8,128)(2,1)S(1)} %attend.3.mine_ref, bf16[512,512]{1,0:T(8,128)(2,1)S(1)} %collective-permute-done.44.other_ref, ...), custom_call_target="tpu_custom_call" | custom-call | flops 2147483648 | bytes 7340032 | tf_op jit(solution)/shard_map/mix/pallas_call | solution.py:255
  155.9 2.3 %mix.3 = (bf16[128,2048]{1,0:T(8,128)(2,1)S(1)}, bf16[128,2048]{1,0:T(8,128)(2,1)S(1)}, bf16[128,2048]{1,0:T(8,128)(2,1)S(1)}, bf16[128,2048]{1,0:T(8,128)(2,1)S(1)}) custom-call(bf16[512,512]{1,0:T(8,128)(2,1)S(1)} %attend.3.mine_ref, bf16[512,512]{1,0:T(8,128)(2,1)S(1)} %collective-permute-done.44.other_ref, ...), custom_call_target="tpu_custom_call" | custom-call | flops 2147483648 | bytes 7340032 | tf_op jit(solution)/shard_map/mix/pallas_call | solution.py:255
  158.3 2.7 %collective-permute-start.54 = (bf16[128,2048]{1,0:T(8,128)(2,1)S(1)}, bf16[128,2048]{1,0:T(8,128)(2,1)S(1)}, u32[]{:S(2)}, u32[]{:S(2)}) collective-permute-start(bf16[128,2048]{1,0:T(8,128)(2,1)S(1)} %get-tuple-element.118), channel_id=1, source_target_pairs={{0,6},{2,0},{4,2},{6,4},{1,7},{3,1},{5,3},{7,5},{8,14},{10,8},{12,... | collective-permute-start | bytes 1572872 | tf_op jit(solution)/shard_map/ppermute | solution.py:23
  162.5 8.2 %collective-permute-done.47 = bf16[128,2048]{1,0:T(8,128)(2,1)S(1)} collective-permute-done((bf16[128,2048]{1,0:T(8,128)(2,1)S(1)}, bf16[128,2048]{1,0:T(8,128)(2,1)S(1)}, u32[]{:S(2)}, u32[]{:S(2)}) %collective-permute-start.47) | collective-permute-done | bytes 524320 | tf_op jit(solution)/shard_map/ppermute | solution.py:23
  172.2 3.5 %collective-permute-start.55 = (bf16[128,2048]{1,0:T(8,128)(2,1)S(1)}, bf16[128,2048]{1,0:T(8,128)(2,1)S(1)}, u32[]{:S(2)}, u32[]{:S(2)}) collective-permute-start(bf16[128,2048]{1,0:T(8,128)(2,1)S(1)} %add_convert_fusion), channel_id=1, source_target_pairs={{0,6},{2,0},{4,2},{6,4},{1,7},{3,1},{5,3},{7,5},{8,14},{10,8},{12,... | collective-permute-start | bytes 1572872 | tf_op jit(solution)/shard_map/ppermute | solution.py:23
  175.6 7.6 %collective-permute-done.49.refs_2_ = bf16[128,2048]{1,0:T(8,128)(2,1)S(1)} collective-permute-done((bf16[128,2048]{1,0:T(8,128)(2,1)S(1)}, bf16[128,2048]{1,0:T(8,128)(2,1)S(1)}, u32[]{:S(2)}, u32[]{:S(2)}) %collective-permute-start.49) | collective-permute-done | bytes 524320 | tf_op jit(solution)/shard_map/ppermute | solution.py:23
  183.3 9.9 %collective-permute-done.48.refs_1_ = bf16[128,2048]{1,0:T(8,128)(2,1)S(1)} collective-permute-done((bf16[128,2048]{1,0:T(8,128)(2,1)S(1)}, bf16[128,2048]{1,0:T(8,128)(2,1)S(1)}, u32[]{:S(2)}, u32[]{:S(2)}) %collective-permute-start.48) | collective-permute-done | bytes 524320 | tf_op jit(solution)/shard_map/ppermute | solution.py:23
  (145 shorter events, 45.5 us)
Async XLA Ops:
  16.0 10.4 %collective-permute-start.6 = (bf16[4,4,16,896]{3,2,1,0:T(8,128)(2,1)S(1)}, bf16[4,4,16,896]{3,2,1,0:T(8,128)(2,1)S(1)}, u32[]{:S(2)}, u32[]{:S(2)}) collective-permute-start(bf16[4,4,16,896]{3,2,1,0:T(8,128)(2,1)S(1)} %pad_maximum_fusion.2), channel_id=1, source_target_pairs={{0,8},{8,16},{16,24},{24,0},{1,9},{9,17},{17,25},{25,1},{2,10},{10... | collective-permute-start | bytes 1376264 | tf_op jit(solution)/shard_map/ppermute | solution.py:23
  16.2 10.9 %collective-permute-start.7 = (bf16[4,4,16,896]{3,2,1,0:T(8,128)(2,1)S(1)}, bf16[4,4,16,896]{3,2,1,0:T(8,128)(2,1)S(1)}, u32[]{:S(2)}, u32[]{:S(2)}) collective-permute-start(bf16[4,4,16,896]{3,2,1,0:T(8,128)(2,1)S(1)} %pad_maximum_fusion.2), channel_id=1, source_target_pairs={{0,24},{8,0},{16,8},{24,16},{1,25},{9,1},{17,9},{25,17},{2,26},{10... | collective-permute-start | bytes 1376264 | tf_op jit(solution)/shard_map/ppermute | solution.py:23
  32.8 14.0 %collective-permute-start.10 = (bf16[256,512]{1,0:T(8,128)(2,1)}, bf16[256,512]{1,0:T(8,128)(2,1)}, u32[]{:S(2)}, u32[]{:S(2)}) collective-permute-start(bf16[256,512]{1,0:T(8,128)(2,1)} %param.15), channel_id=1, source_target_pairs={{0,8},{8,16},{16,24},{24,0},{1,9},{9,17},{17,25},{25,1},{2,10},{10... | collective-permute-start | bytes 786440 | tf_op jit(solution)/shard_map/ppermute | solution.py:23
  32.8 9.9 %collective-permute-start.19 = (bf16[2,4,16,896]{3,2,1,0:T(8,128)(2,1)}, bf16[2,4,16,896]{3,2,1,0:T(8,128)(2,1)S(1)}, u32[]{:S(2)}, u32[]{:S(2)}) collective-permute-start(bf16[2,4,16,896]{3,2,1,0:T(8,128)(2,1)} %slice.56), channel_id=1, source_target_pairs={{0,8},{8,16},{16,24},{24,0},{1,9},{9,17},{17,25},{25,1},{2,10},{10... | collective-permute-start | bytes 688136 | tf_op jit(solution)/shard_map/ppermute | solution.py:23
  42.7 10.1 %collective-permute-start.11 = (bf16[256,512]{1,0:T(8,128)(2,1)}, bf16[256,512]{1,0:T(8,128)(2,1)}, u32[]{:S(2)}, u32[]{:S(2)}) collective-permute-start(bf16[256,512]{1,0:T(8,128)(2,1)} %param.15), channel_id=1, source_target_pairs={{0,24},{8,0},{16,8},{24,16},{1,25},{9,1},{17,9},{25,17},{2,26},{10... | collective-permute-start | bytes 786440 | tf_op jit(solution)/shard_map/ppermute | solution.py:23
  44.3 10.7 %collective-permute-start.14 = (bf16[512,256]{1,0:T(8,128)(2,1)}, bf16[512,256]{1,0:T(8,128)(2,1)}, u32[]{:S(2)}, u32[]{:S(2)}) collective-permute-start(bf16[512,256]{1,0:T(8,128)(2,1)} %param.18), channel_id=1, source_target_pairs={{0,96},{32,0},{64,32},{96,64},{1,97},{33,1},{65,33},{97,65},{2,98}... | collective-permute-start | bytes 786440 | tf_op jit(solution)/shard_map/ppermute | solution.py:23
  55.2 11.4 %collective-permute-start.28 = (bf16[4,56,1024]{2,1,0:T(8,128)(2,1)S(1)}, bf16[4,56,1024]{2,1,0:T(8,128)(2,1)S(1)}, u32[]{:S(2)}, u32[]{:S(2)}) collective-permute-start(bf16[4,56,1024]{2,1,0:T(8,128)(2,1)S(1)} %pad_maximum_fusion.4.refs_0_), channel_id=1, source_target_pairs={{0,24},{8,0},{16,8},{24,16},{1,25},{9,1},{17,9},{25,17},{2,26},{10... | collective-permute-start | bytes 1376264 | tf_op jit(solution)/shard_map/ppermute | solution.py:23
  57.9 22.9 %collective-permute-start.25 = (bf16[32,16,896]{2,1,0:T(8,128)(2,1)S(1)}, bf16[32,16,896]{2,1,0:T(8,128)(2,1)S(1)}, u32[]{:S(2)}, u32[]{:S(2)}) collective-permute-start(bf16[32,16,896]{2,1,0:T(8,128)(2,1)S(1)} %pick.1.refs_0_), channel_id=1, source_target_pairs={{0,2},{2,4},{4,6},{6,0},{1,3},{3,5},{5,7},{7,1},{8,10},{10,12},{12... | collective-permute-start | bytes 2752520 | tf_op jit(solution)/shard_map/ppermute | solution.py:23
  60.5 26.2 %collective-permute-start.23 = (bf16[4,256,512]{2,1,0:T(8,128)(2,1)S(1)}, bf16[4,256,512]{2,1,0:T(8,128)(2,1)S(1)}, u32[]{:S(2)}, u32[]{:S(2)}) collective-permute-start(bf16[4,256,512]{2,1,0:T(8,128)(2,1)S(1)} %pad_maximum_fusion.refs_0_), channel_id=1, source_target_pairs={{0,32},{32,64},{64,96},{96,0},{1,33},{33,65},{65,97},{97,1},{2,34}... | collective-permute-start | bytes 3145736 | tf_op jit(solution)/shard_map/ppermute | solution.py:23
  61.8 24.9 %collective-permute-start.24 = (bf16[4,256,512]{2,1,0:T(8,128)(2,1)S(1)}, bf16[4,256,512]{2,1,0:T(8,128)(2,1)S(1)}, u32[]{:S(2)}, u32[]{:S(2)}) collective-permute-start(bf16[4,256,512]{2,1,0:T(8,128)(2,1)S(1)} %pad_maximum_fusion.refs_0_), channel_id=1, source_target_pairs={{0,96},{32,0},{64,32},{96,64},{1,97},{33,1},{65,33},{97,65},{2,98}... | collective-permute-start | bytes 3145736 | tf_op jit(solution)/shard_map/ppermute | solution.py:23
  64.2 22.4 %collective-permute-start.26 = (bf16[32,16,896]{2,1,0:T(8,128)(2,1)S(1)}, bf16[32,16,896]{2,1,0:T(8,128)(2,1)S(1)}, u32[]{:S(2)}, u32[]{:S(2)}) collective-permute-start(bf16[32,16,896]{2,1,0:T(8,128)(2,1)S(1)} %pick.1.refs_0_), channel_id=1, source_target_pairs={{0,6},{2,0},{4,2},{6,4},{1,7},{3,1},{5,3},{7,5},{8,14},{10,8},{12,... | collective-permute-start | bytes 2752520 | tf_op jit(solution)/shard_map/ppermute | solution.py:23
  80.8 35.4 %collective-permute-start.35 = (bf16[4,512,256]{2,1,0:T(8,128)(2,1)S(1)}, bf16[4,512,256]{2,1,0:T(8,128)(2,1)S(1)}, u32[]{:S(2)}, u32[]{:S(2)}) collective-permute-start(bf16[4,512,256]{2,1,0:T(8,128)(2,1)S(1)} %pad_maximum_fusion.1.refs_0_), channel_id=1, source_target_pairs={{0,8},{8,16},{16,24},{24,0},{1,9},{9,17},{17,25},{25,1},{2,10},{10... | collective-permute-start | bytes 3145736 | tf_op jit(solution)/shard_map/ppermute | solution.py:23
  80.8 35.4 %collective-permute-start.36 = (bf16[4,512,256]{2,1,0:T(8,128)(2,1)S(1)}, bf16[4,512,256]{2,1,0:T(8,128)(2,1)S(1)}, u32[]{:S(2)}, u32[]{:S(2)}) collective-permute-start(bf16[4,512,256]{2,1,0:T(8,128)(2,1)S(1)} %pad_maximum_fusion.1.refs_0_), channel_id=1, source_target_pairs={{0,24},{8,0},{16,8},{24,16},{1,25},{9,1},{17,9},{25,17},{2,26},{10... | collective-permute-start | bytes 3145736 | tf_op jit(solution)/shard_map/ppermute | solution.py:23
  86.8 11.5 %collective-permute-start.34 = (bf16[16,16,896]{2,1,0:T(8,128)(2,1)S(1)}, bf16[16,16,896]{2,1,0:T(8,128)(2,1)S(1)}, u32[]{:S(2)}, u32[]{:S(2)}) collective-permute-start(bf16[16,16,896]{2,1,0:T(8,128)(2,1)S(1)} %slice.61), channel_id=1, source_target_pairs={{0,6},{2,0},{4,2},{6,4},{1,7},{3,1},{5,3},{7,5},{8,14},{10,8},{12,... | collective-permute-start | bytes 1376264 | tf_op jit(solution)/shard_map/ppermute | solution.py:23
  89.5 27.3 %collective-permute-start.31 = (bf16[2,256,512]{2,1,0:T(8,128)(2,1)S(1)}, bf16[2,256,512]{2,1,0:T(8,128)(2,1)S(1)}, u32[]{:S(2)}, u32[]{:S(2)}) collective-permute-start(bf16[2,256,512]{2,1,0:T(8,128)(2,1)S(1)} %slice.62), channel_id=1, source_target_pairs={{0,32},{32,64},{64,96},{96,0},{1,33},{33,65},{65,97},{97,1},{2,34}... | collective-permute-start | bytes 1572872 | tf_op jit(solution)/shard_map/ppermute | solution.py:23
  95.4 21.6 %collective-permute-start.32 = (bf16[2,256,512]{2,1,0:T(8,128)(2,1)S(1)}, bf16[2,256,512]{2,1,0:T(8,128)(2,1)S(1)}, u32[]{:S(2)}, u32[]{:S(2)}) collective-permute-start(bf16[2,256,512]{2,1,0:T(8,128)(2,1)S(1)} %slice.63), channel_id=1, source_target_pairs={{0,96},{32,0},{64,32},{96,64},{1,97},{33,1},{65,33},{97,65},{2,98}... | collective-permute-start | bytes 1572872 | tf_op jit(solution)/shard_map/ppermute | solution.py:23
  98.4 34.1 %collective-permute-start.37 = (bf16[32,16,896]{2,1,0:T(8,128)(2,1)S(1)}, bf16[32,16,896]{2,1,0:T(8,128)(2,1)S(1)}, u32[]{:S(2)}, u32[]{:S(2)}) collective-permute-start(bf16[32,16,896]{2,1,0:T(8,128)(2,1)S(1)} %pick.1.refs_0_), channel_id=1, source_target_pairs={{0,1},{1,0},{2,3},{3,2},{4,5},{5,4},{6,7},{7,6},{8,9},{9,8},{10,11... | collective-permute-start | bytes 2752520 | tf_op jit(solution)/shard_map/ppermute | solution.py:23
  116.2 16.2 %collective-permute-start.38 = (bf16[32,16,896]{2,1,0:T(8,128)(2,1)S(1)}, bf16[32,16,896]{2,1,0:T(8,128)(2,1)S(1)}, u32[]{:S(2)}, u32[]{:S(2)}) collective-permute-start(bf16[32,16,896]{2,1,0:T(8,128)(2,1)S(1)} %collective-permute-done.25.refs_1_), channel_id=1, source_target_pairs={{0,1},{1,0},{2,3},{3,2},{4,5},{5,4},{6,7},{7,6},{8,9},{9,8},{10,11... | collective-permute-start | bytes 2752520 | tf_op jit(solution)/shard_map/ppermute | solution.py:23
  116.3 16.1 %collective-permute-start.39 = (bf16[32,16,896]{2,1,0:T(8,128)(2,1)S(1)}, bf16[32,16,896]{2,1,0:T(8,128)(2,1)S(1)}, u32[]{:S(2)}, u32[]{:S(2)}) collective-permute-start(bf16[32,16,896]{2,1,0:T(8,128)(2,1)S(1)} %collective-permute-done.26.refs_2_), channel_id=1, source_target_pairs={{0,1},{1,0},{2,3},{3,2},{4,5},{5,4},{6,7},{7,6},{8,9},{9,8},{10,11... | collective-permute-start | bytes 2752520 | tf_op jit(solution)/shard_map/ppermute | solution.py:23
  116.8 12.9 %collective-permute-start.40 = (bf16[16,16,896]{2,1,0:T(8,128)(2,1)S(1)}, bf16[16,16,896]{2,1,0:T(8,128)(2,1)S(1)}, u32[]{:S(2)}, u32[]{:S(2)}) collective-permute-start(bf16[16,16,896]{2,1,0:T(8,128)(2,1)S(1)} %collective-permute-done.33.refs_3_), channel_id=1, source_target_pairs={{0,1},{1,0},{2,3},{3,2},{4,5},{5,4},{6,7},{7,6},{8,9},{9,8},{10,11... | collective-permute-start | bytes 1376264 | tf_op jit(solution)/shard_map/ppermute | solution.py:23
  117.0 12.8 %collective-permute-start.41 = (bf16[16,16,896]{2,1,0:T(8,128)(2,1)S(1)}, bf16[16,16,896]{2,1,0:T(8,128)(2,1)S(1)}, u32[]{:S(2)}, u32[]{:S(2)}) collective-permute-start(bf16[16,16,896]{2,1,0:T(8,128)(2,1)S(1)} %collective-permute-done.34.refs_4_), channel_id=1, source_target_pairs={{0,1},{1,0},{2,3},{3,2},{4,5},{5,4},{6,7},{7,6},{8,9},{9,8},{10,11... | collective-permute-start | bytes 1376264 | tf_op jit(solution)/shard_map/ppermute | solution.py:23
  129.7 14.9 %collective-permute-start.42 = (bf16[2,512,256]{2,1,0:T(8,128)(2,1)S(1)}, bf16[2,512,256]{2,1,0:T(8,128)(2,1)S(1)}, u32[]{:S(2)}, u32[]{:S(2)}) collective-permute-start(bf16[2,512,256]{2,1,0:T(8,128)(2,1)S(1)} %slice.66), channel_id=1, source_target_pairs={{0,8},{8,16},{16,24},{24,0},{1,9},{9,17},{17,25},{25,1},{2,10},{10... | collective-permute-start | bytes 1572872 | tf_op jit(solution)/shard_map/ppermute | solution.py:23
  129.8 14.8 %collective-permute-start.43 = (bf16[2,512,256]{2,1,0:T(8,128)(2,1)S(1)}, bf16[2,512,256]{2,1,0:T(8,128)(2,1)S(1)}, u32[]{:S(2)}, u32[]{:S(2)}) collective-permute-start(bf16[2,512,256]{2,1,0:T(8,128)(2,1)S(1)} %slice.67), channel_id=1, source_target_pairs={{0,24},{8,0},{16,8},{24,16},{1,25},{9,1},{17,9},{25,17},{2,26},{10... | collective-permute-start | bytes 1572872 | tf_op jit(solution)/shard_map/ppermute | solution.py:23
  145.3 10.6 %collective-permute-start.50 = (bf16[4,512,256]{2,1,0:T(8,128)(2,1)S(1)}, bf16[4,512,256]{2,1,0:T(8,128)(2,1)S(1)}, u32[]{:S(2)}, u32[]{:S(2)}) collective-permute-start(bf16[4,512,256]{2,1,0:T(8,128)(2,1)S(1)} %collective-permute-done.36.refs_0_), channel_id=1, source_target_pairs={{0,1},{1,0},{2,3},{3,2},{4,5},{5,4},{6,7},{7,6},{8,9},{9,8},{10,11... | collective-permute-start | bytes 3145736 | tf_op jit(solution)/shard_map/ppermute | solution.py:23
  145.8 10.1 %collective-permute-start.51 = (bf16[2,512,256]{2,1,0:T(8,128)(2,1)S(1)}, bf16[2,512,256]{2,1,0:T(8,128)(2,1)S(1)}, u32[]{:S(2)}, u32[]{:S(2)}) collective-permute-start(bf16[2,512,256]{2,1,0:T(8,128)(2,1)S(1)} %collective-permute-done.42.refs_1_), channel_id=1, source_target_pairs={{0,1},{1,0},{2,3},{3,2},{4,5},{5,4},{6,7},{7,6},{8,9},{9,8},{10,11... | collective-permute-start | bytes 1572872 | tf_op jit(solution)/shard_map/ppermute | solution.py:23
  145.8 10.1 %collective-permute-start.52 = (bf16[2,512,256]{2,1,0:T(8,128)(2,1)S(1)}, bf16[2,512,256]{2,1,0:T(8,128)(2,1)S(1)}, u32[]{:S(2)}, u32[]{:S(2)}) collective-permute-start(bf16[2,512,256]{2,1,0:T(8,128)(2,1)S(1)} %collective-permute-done.43.refs_2_), channel_id=1, source_target_pairs={{0,1},{1,0},{2,3},{3,2},{4,5},{5,4},{6,7},{7,6},{8,9},{9,8},{10,11... | collective-permute-start | bytes 1572872 | tf_op jit(solution)/shard_map/ppermute | solution.py:23
  155.6 15.1 %collective-permute-start.47 = (bf16[128,2048]{1,0:T(8,128)(2,1)S(1)}, bf16[128,2048]{1,0:T(8,128)(2,1)S(1)}, u32[]{:S(2)}, u32[]{:S(2)}) collective-permute-start(bf16[128,2048]{1,0:T(8,128)(2,1)S(1)} %get-tuple-element.109), channel_id=1, source_target_pairs={{0,2},{2,4},{4,6},{6,0},{1,3},{3,5},{5,7},{7,1},{8,10},{10,12},{12... | collective-permute-start | bytes 1572872 | tf_op jit(solution)/shard_map/ppermute | solution.py:23
  158.3 13.7 %collective-permute-start.54 = (bf16[128,2048]{1,0:T(8,128)(2,1)S(1)}, bf16[128,2048]{1,0:T(8,128)(2,1)S(1)}, u32[]{:S(2)}, u32[]{:S(2)}) collective-permute-start(bf16[128,2048]{1,0:T(8,128)(2,1)S(1)} %get-tuple-element.118), channel_id=1, source_target_pairs={{0,6},{2,0},{4,2},{6,4},{1,7},{3,1},{5,3},{7,5},{8,14},{10,8},{12,... | collective-permute-start | bytes 1572872 | tf_op jit(solution)/shard_map/ppermute | solution.py:23
  161.0 22.3 %collective-permute-start.49 = (bf16[128,2048]{1,0:T(8,128)(2,1)S(1)}, bf16[128,2048]{1,0:T(8,128)(2,1)S(1)}, u32[]{:S(2)}, u32[]{:S(2)}) collective-permute-start(bf16[128,2048]{1,0:T(8,128)(2,1)S(1)} %get-tuple-element.110), channel_id=1, source_target_pairs={{0,6},{2,0},{4,2},{6,4},{1,7},{3,1},{5,3},{7,5},{8,14},{10,8},{12,... | collective-permute-start | bytes 1572872 | tf_op jit(solution)/shard_map/ppermute | solution.py:23
  161.1 22.2 %collective-permute-start.53 = (bf16[128,2048]{1,0:T(8,128)(2,1)S(1)}, bf16[128,2048]{1,0:T(8,128)(2,1)S(1)}, u32[]{:S(2)}, u32[]{:S(2)}) collective-permute-start(bf16[128,2048]{1,0:T(8,128)(2,1)S(1)} %get-tuple-element.116), channel_id=1, source_target_pairs={{0,2},{2,4},{4,6},{6,0},{1,3},{3,5},{5,7},{7,1},{8,10},{10,12},{12... | collective-permute-start | bytes 1572872 | tf_op jit(solution)/shard_map/ppermute | solution.py:23
  170.8 22.3 %collective-permute-start.48 = (bf16[128,2048]{1,0:T(8,128)(2,1)S(1)}, bf16[128,2048]{1,0:T(8,128)(2,1)S(1)}, u32[]{:S(2)}, u32[]{:S(2)}) collective-permute-start(bf16[128,2048]{1,0:T(8,128)(2,1)S(1)} %add_convert_fusion.1), channel_id=1, source_target_pairs={{0,2},{2,4},{4,6},{6,0},{1,3},{3,5},{5,7},{7,1},{8,10},{10,12},{12... | collective-permute-start | bytes 1572872 | tf_op jit(solution)/shard_map/ppermute | solution.py:23
  172.2 22.3 %collective-permute-start.55 = (bf16[128,2048]{1,0:T(8,128)(2,1)S(1)}, bf16[128,2048]{1,0:T(8,128)(2,1)S(1)}, u32[]{:S(2)}, u32[]{:S(2)}) collective-permute-start(bf16[128,2048]{1,0:T(8,128)(2,1)S(1)} %add_convert_fusion), channel_id=1, source_target_pairs={{0,6},{2,0},{4,2},{6,4},{1,7},{3,1},{5,3},{7,5},{8,14},{10,8},{12,... | collective-permute-start | bytes 1572872 | tf_op jit(solution)/shard_map/ppermute | solution.py:23
  (38 other events, 451.7 us)
